TPU v7x, 1024 devices: a whole 4x4x32 slice. The times are simulated.
1024 devices in a mesh: pipe: 128 (over y_hi, z, core), dp: 8 (over x, y_lo).
Axes of the slice: x: 4, y: 4 (y_hi: 2, y_lo: 2; y = y_hi * 2 + y_lo), z: 32, core: 2. Of those that a mesh axis runs over, the one named last changes fastest.
Arguments:
- forward_state: bfloat16 [2, 128, 128, 3584], P(None, 'pipe', 'dp'), may hold values from -6 to 6
- backward_state: bfloat16 [2, 128, 128, 3584], P(None, 'pipe', 'dp'), may hold values from -1.5 to 1.5
- stored_inputs: bfloat16 [2, 128, 2, 128, 3584], P(None, 'pipe', None, 'dp'), may hold values from -6 to 6
- down_weight: bfloat16 [128, 2, 3584, 256], P('pipe'), may hold values from -0.09375 to 0.09375
- up_weight: bfloat16 [128, 2, 256, 3584], P('pipe'), may hold values from -0.375 to 0.375
- norm_gain: float32 [128, 2, 3584], P('pipe'), may hold values from 0.25 to 1.75
- latent_gain: float32 [128, 2, 2, 256], P('pipe'), may hold values from 0.25 to 1.75
- forward_lengths: int32 [2, 128, 4, 8], P(None, 'pipe', None, 'dp'), may hold values from 1 to 16
- stored_lengths: int32 [2, 128, 2, 8], P(None, 'pipe', None, 'dp'), may hold values from 1 to 16
- plan: int32 [2, 128, 4], P(None, 'pipe'), may hold values from 0 to 1
Outputs:
- forward_out: bfloat16 [2, 128, 128, 3584], P(None, 'pipe', 'dp')
- backward_out: bfloat16 [2, 128, 128, 3584], P(None, 'pipe', 'dp')
- grad_down: float32 [128, 3584, 256], P('pipe', 'dp')
Inputs may be any that keep to these rules, and one draw needn't show every extreme that they name: `forward_lengths`: valid tokens of a forward micro-batch. `stored_lengths`: valid tokens of a stored micro-batch. `plan`: a slot of the stored inputs.
All inputs are finite; a program needn't handle non-finite values.
Results may differ from a plain program's by a relative error of at most 0.027.
Values may be sent and summed in bfloat16 or wider, within the bound.
No kernel may reach another device: no remote copies, remote signals or barrier semaphores. Data moves between devices by JAX's collectives and lax.ppermute only.
A program may use at most 64 MiB of HBM per device.

v0:
```python
import jax
import jax.numpy as jnp
from jax import lax
from jax.sharding import PartitionSpec as P

epsilon = 1e-06
score_factor = 2.0


def passed_along(shard, axis, by):
    size = lax.axis_size(axis)
    pairs = [(i, i + by) for i in range(size) if 0 <= i + by < size]
    return lax.ppermute(shard, axis, pairs)


def swapped(block, axis, stride):
    count = lax.axis_size(axis)
    route = []
    for low in range(count):
        high = low | 1 << stride
        if high != low and high < count:
            route += [(low, high), (high, low)]
    return lax.ppermute(block, axis, route)


def round_through(values):
    rounded = values.astype(jnp.bfloat16).astype(jnp.float32)
    return values + lax.stop_gradient(rounded - values)


def normed_input(inputs_float, gain_vector):
    inverse = lax.rsqrt(jnp.mean(inputs_float * inputs_float, axis=-1, keepdims=True) + epsilon)
    return inputs_float * inverse * gain_vector


def attend(latent, latent_gain, length):
    row_count = latent.shape[1]
    inverse = lax.rsqrt(jnp.mean(latent * latent, axis=-1, keepdims=True) + epsilon)
    key_rows = round_through(latent * inverse * latent_gain[0])
    query_rows = round_through(latent * inverse * latent_gain[1])
    scores = jnp.einsum("gic,gjc->gij", query_rows, key_rows, precision=lax.Precision.HIGHEST) * (
        score_factor / latent.shape[2]
    )
    position = jnp.arange(row_count)
    visible = (position[None, None, :] <= position[None, :, None]) & (
        position[None, None, :] < length[:, None, None]
    )
    weights = jnp.where(visible, jnp.exp(scores), 0.0)
    probabilities = round_through(weights / jnp.sum(weights, axis=-1, keepdims=True))
    return round_through(
        jnp.einsum("gij,gjc->gic", probabilities, key_rows, precision=lax.Precision.HIGHEST)
    )


def contract_last(left, right):
    return lax.dot_general(
        left, right, (((1,), (1,)), ((), ())), preferred_element_type=jnp.float32
    )


def side_work(
    forward_rows,
    stored_rows,
    grad_out,
    w_down,
    w_up,
    gain_vector,
    latent_gain,
    forward_length,
    stored_length,
):
    row_count = forward_rows.shape[0]
    forward_float = forward_rows.astype(jnp.float32)
    stored_float = stored_rows.astype(jnp.float32)
    normed_forward = normed_input(forward_float, gain_vector).astype(jnp.bfloat16)
    normed_stored = normed_input(stored_float, gain_vector).astype(jnp.bfloat16)
    latent_both = jnp.dot(
        jnp.concatenate([normed_forward, normed_stored], axis=0),
        w_down,
        preferred_element_type=jnp.float32,
    )
    latent_forward = latent_both[:row_count]
    latent_stored = latent_both[row_count:]
    mixed_rows = attend(latent_forward[None], latent_gain, forward_length[None])[0].astype(
        jnp.bfloat16
    )
    output_rows = (
        forward_float + jnp.dot(mixed_rows, w_up, preferred_element_type=jnp.float32)
    ).astype(jnp.bfloat16)
    grad_mixed = contract_last(grad_out, w_up)
    _, pull_latent = jax.vjp(
        lambda latent_rows: attend(latent_rows, latent_gain, stored_length[None]),
        latent_stored[None],
    )
    grad_latent = pull_latent(grad_mixed[None])[0][0].astype(jnp.bfloat16)
    grad_normed = contract_last(grad_latent, w_down)
    _, pull_norm = jax.vjp(lambda values: normed_input(values, gain_vector), stored_float)
    grad_input = (grad_out.astype(jnp.float32) + pull_norm(grad_normed)[0]).astype(jnp.bfloat16)
    return (output_rows, grad_input, normed_stored, grad_latent)


def shards(
    forward_state,
    backward_state,
    stored_inputs,
    down_weight,
    up_weight,
    norm_gain,
    latent_gain,
    forward_lengths,
    stored_lengths,
    plan,
):
    features = forward_state.shape[3]
    tick_count = forward_lengths.shape[2]
    forward = [forward_state[0, 0], forward_state[1, 0]]
    backward = [backward_state[0, 0], backward_state[1, 0]]
    kept_normed = [[], []]
    kept_grads = [[], []]

    def run_side(side_index, step_index):
        slot_index = plan[side_index, 0, step_index]
        chosen = lax.dynamic_index_in_dim(
            stored_inputs[side_index, 0], slot_index, 0, keepdims=False
        )
        length = lax.dynamic_index_in_dim(
            stored_lengths[side_index, 0], slot_index, 0, keepdims=False
        )
        output_rows, grad_input, normed, grad_latent = side_work(
            forward[side_index],
            chosen,
            backward[side_index],
            down_weight[0, side_index],
            up_weight[0, side_index],
            norm_gain[0, side_index],
            latent_gain[0, side_index],
            forward_lengths[side_index, 0, step_index, 0],
            length[0],
        )
        kept_normed[side_index].append(normed)
        kept_grads[side_index].append(grad_latent)
        return (output_rows, grad_input)

    for step_index in range(tick_count):
        output_lower, cotangent_lower = run_side(0, step_index)
        next_lower = passed_along(output_lower, "pipe", 1)
        back_lower = passed_along(cotangent_lower, "pipe", -1)
        output_upper, cotangent_upper = run_side(1, step_index)
        next_upper = passed_along(output_upper, "pipe", -1)
        back_upper = passed_along(cotangent_upper, "pipe", 1)
        forward = [next_lower, next_upper]
        backward = [back_lower, back_upper]
    upper_factors = jnp.concatenate(
        [jnp.concatenate(kept_normed[1], axis=0), jnp.concatenate(kept_grads[1], axis=0)], axis=1
    )
    bit_list = list(range(lax.axis_size("pipe").bit_length() - 1))
    for bit_index in bit_list:
        upper_factors = swapped(upper_factors, "pipe", bit_index)
    normed_both = jnp.concatenate(
        [jnp.concatenate(kept_normed[0], axis=0), upper_factors[:, :features]], axis=0
    )
    grads_both = jnp.concatenate(
        [jnp.concatenate(kept_grads[0], axis=0), upper_factors[:, features:]], axis=0
    )
    partial_value = lax.dot_general(
        normed_both, grads_both, (((0,), (0,)), ((), ())), preferred_element_type=jnp.float32
    )
    grad_down = lax.psum_scatter(
        lax.optimization_barrier(partial_value.astype(jnp.bfloat16))
        .astype(jnp.float32)
        .astype(jnp.bfloat16),
        "dp",
        scatter_dimension=0,
        tiled=True,
    ).astype(jnp.float32)
    return (jnp.stack(forward)[:, None], jnp.stack(backward)[:, None], grad_down[None])


def solution(mesh):
    in_specs = (
        P(None, "pipe", "dp", None),
        P(None, "pipe", "dp", None),
        P(None, "pipe", None, "dp", None),
        P("pipe", None, None, None),
        P("pipe", None, None, None),
        P("pipe", None, None),
        P("pipe", None, None, None),
        P(None, "pipe", None, "dp"),
        P(None, "pipe", None, "dp"),
        P(None, "pipe", None),
    )
    out_specs = (P(None, "pipe", "dp", None), P(None, "pipe", "dp", None), P("pipe", "dp", None))
    return jax.shard_map(shards, mesh=mesh, in_specs=in_specs, out_specs=out_specs, check_vma=False)
```

profile of v0, /device:TPU:24, one launch (start us, length us, event | category | flops | bytes accessed | tf_op | source)
XLA Modules:
  0.0 527.4 jit_solution(1390349906146785228)
XLA Ops:
  7.2 1.5 fusion.559
  19.0 0.7 fusion.560
  19.7 1.1 fusion.162
  20.8 1.5 fusion.558
  28.1 0.7 constant_dynamic-slice_fusion
  28.8 1.0 iota_compare_fusion.4
  29.8 0.8 fusion.557
  30.6 0.9 slice_reduce_fusion.1
  31.5 1.1 fusion.556
  32.7 1.1 fusion.164
  33.9 1.9 fusion.30
  38.2 18.8 %collective-permute-start.4 = (bf16[16,3584]{1,0:T(8,128)(2,1)S(1)}, bf16[16,3584]{1,0:T(8,128)(2,1)S(1)}, u32[]{:S(2)}, u32[]{:S(2)}) collective-permute-start(bf16[16,3584]{1,0:T(8,128)(2,1)S(1)} %fusion.4), channel_id=1, source_target_pairs={{8,0},{16,8},{24,16},{32,24},{40,32},{48,40},{56,48},{64,56},{72,6... | collective-permute-start | bytes 344072 | tf_op jit(solution)/shard_map/ppermute | solution.py:13
  61.4 1.9 collective-permute-start
  63.8 0.7 iota_compare_fusion.13
  67.6 0.7 iota_compare_fusion.1
  69.6 0.7 iota_compare_fusion.7
  70.7 0.7 fusion.187
  71.8 0.7 fusion.171
  73.3 0.7 iota_compare_fusion.5
  76.0 7.3 %collective-permute-start.8 = (bf16[16,3584]{1,0:T(8,128)(2,1)S(1)}, bf16[16,3584]{1,0:T(8,128)(2,1)S(1)}, u32[]{:S(2)}, u32[]{:S(2)}) collective-permute-start(bf16[16,3584]{1,0:T(8,128)(2,1)S(1)} %get-tuple-element.56), channel_id=1, source_target_pairs={{8,0},{16,8},{24,16},{32,24},{40,32},{48,40},{56,48},{64,56},{72,6... | collective-permute-start | bytes 344072 | tf_op jit(solution)/shard_map/ppermute | solution.py:13
  83.3 1.9 collective-permute-start.12
  87.0 5.9 %collective-permute-done.12 = bf16[16,3584]{1,0:T(8,128)(2,1)S(1)} collective-permute-done((bf16[16,3584]{1,0:T(8,128)(2,1)S(1)}, bf16[16,3584]{1,0:T(8,128)(2,1)S(1)}, u32[]{:S(2)}, u32[]{:S(2)}) %collective-permute-start.12) | collective-permute-done | bytes 114720 | tf_op jit(solution)/shard_map/ppermute | solution.py:13
  95.6 1.9 collective-permute-start.1
  98.7 7.3 %collective-permute-start.5 = (bf16[16,3584]{1,0:T(8,128)(2,1)S(1)}, bf16[16,3584]{1,0:T(8,128)(2,1)S(1)}, u32[]{:S(2)}, u32[]{:S(2)}) collective-permute-start(bf16[16,3584]{1,0:T(8,128)(2,1)S(1)} %fusion.5), channel_id=1, source_target_pairs={{8,0},{16,8},{24,16},{32,24},{40,32},{48,40},{56,48},{64,56},{72,6... | collective-permute-start | bytes 344072 | tf_op jit(solution)/shard_map/ppermute | solution.py:13
  106.0 0.7 fusion.175
  106.9 1.9 collective-permute-start.9
  108.9 0.7 fusion.191
  113.9 2.1 collective-permute-start.2
  116.1 0.7 fusion.179
  117.0 7.2 %collective-permute-start.10 = (bf16[16,3584]{1,0:T(8,128)(2,1)S(1)}, bf16[16,3584]{1,0:T(8,128)(2,1)S(1)}, u32[]{:S(2)}, u32[]{:S(2)}) collective-permute-start(bf16[16,3584]{1,0:T(8,128)(2,1)S(1)} %fusion.151), channel_id=1, source_target_pairs={{8,0},{16,8},{24,16},{32,24},{40,32},{48,40},{56,48},{64,56},{72,6... | collective-permute-start | bytes 344072 | tf_op jit(solution)/shard_map/ppermute | solution.py:13
  125.0 1.9 collective-permute-start.13
  127.2 7.4 %collective-permute-done.13 = bf16[16,3584]{1,0:T(8,128)(2,1)S(1)} collective-permute-done((bf16[16,3584]{1,0:T(8,128)(2,1)S(1)}, bf16[16,3584]{1,0:T(8,128)(2,1)S(1)}, u32[]{:S(2)}, u32[]{:S(2)}) %collective-permute-start.13) | collective-permute-done | bytes 114720 | tf_op jit(solution)/shard_map/ppermute | solution.py:13
  137.4 2.1 collective-permute-start.6
  139.7 0.7 fusion.195
  140.5 1.2 collective-permute-done.6
  142.6 1.9 collective-permute-start.14
  144.8 7.7 %collective-permute-done.14 = bf16[16,3584]{1,0:T(8,128)(2,1)S(1)} collective-permute-done((bf16[16,3584]{1,0:T(8,128)(2,1)S(1)}, bf16[16,3584]{1,0:T(8,128)(2,1)S(1)}, u32[]{:S(2)}, u32[]{:S(2)}) %collective-permute-start.14) | collective-permute-done | bytes 114720 | tf_op jit(solution)/shard_map/ppermute | solution.py:13
  154.4 1.9 collective-permute-start.16
  156.8 1.3 collective-permute-done.16
  158.1 1.9 collective-permute-start.17
  160.8 12.4 %collective-permute-done.17 = bf16[64,3840]{1,0:T(8,128)(2,1)S(1)} collective-permute-done((bf16[64,3840]{1,0:T(8,128)(2,1)S(1)}, bf16[64,3840]{1,0:T(8,128)(2,1)S(1)}, u32[]{:S(2)}, u32[]{:S(2)}) %collective-permute-start.17) | collective-permute-done | bytes 491552 | tf_op jit(solution)/shard_map/ppermute | solution.py:23
  173.3 1.9 collective-permute-start.18
  175.8 23.2 %collective-permute-done.18 = bf16[64,3840]{1,0:T(8,128)(2,1)S(1)} collective-permute-done((bf16[64,3840]{1,0:T(8,128)(2,1)S(1)}, bf16[64,3840]{1,0:T(8,128)(2,1)S(1)}, u32[]{:S(2)}, u32[]{:S(2)}) %collective-permute-start.18) | collective-permute-done | bytes 491552 | tf_op jit(solution)/shard_map/ppermute | solution.py:23
  199.0 1.9 collective-permute-start.19
  201.4 46.8 %collective-permute-done.19 = bf16[64,3840]{1,0:T(8,128)(2,1)S(1)} collective-permute-done((bf16[64,3840]{1,0:T(8,128)(2,1)S(1)}, bf16[64,3840]{1,0:T(8,128)(2,1)S(1)}, u32[]{:S(2)}, u32[]{:S(2)}) %collective-permute-start.19) | collective-permute-done | bytes 491552 | tf_op jit(solution)/shard_map/ppermute | solution.py:23
  248.2 1.9 collective-permute-start.20
  250.7 119.4 %collective-permute-done.20 = bf16[64,3840]{1,0:T(8,128)(2,1)S(1)} collective-permute-done((bf16[64,3840]{1,0:T(8,128)(2,1)S(1)}, bf16[64,3840]{1,0:T(8,128)(2,1)S(1)}, u32[]{:S(2)}, u32[]{:S(2)}) %collective-permute-start.20) | collective-permute-done | bytes 491552 | tf_op jit(solution)/shard_map/ppermute | solution.py:23
  370.0 1.9 collective-permute-start.21
  372.3 1.9 collective-permute-start.3
  374.3 42.8 %collective-permute-done.21 = bf16[64,3840]{1,0:T(8,128)(2,1)S(1)} collective-permute-done((bf16[64,3840]{1,0:T(8,128)(2,1)S(1)}, bf16[64,3840]{1,0:T(8,128)(2,1)S(1)}, u32[]{:S(2)}, u32[]{:S(2)}) %collective-permute-start.21) | collective-permute-done | bytes 491552 | tf_op jit(solution)/shard_map/ppermute | solution.py:23
  417.1 24.4 %collective-permute-start.22 = (bf16[64,3840]{1,0:T(8,128)(2,1)S(1)}, bf16[64,3840]{1,0:T(8,128)(2,1)S(1)}, u32[]{:S(2)}, u32[]{:S(2)}) collective-permute-start(bf16[64,3840]{1,0:T(8,128)(2,1)S(1)} %collective-permute-done.21), channel_id=1, source_target_pairs={{0,512},{512,0},{8,520},{520,8},{16,528},{528,16},{24,536},{536,24... | collective-permute-start | bytes 1474568 | tf_op jit(solution)/shard_map/ppermute | solution.py:23
  441.5 0.7 fusion.183
  442.2 9.2 %collective-permute-done.22 = bf16[64,3840]{1,0:T(8,128)(2,1)S(1)} collective-permute-done((bf16[64,3840]{1,0:T(8,128)(2,1)S(1)}, bf16[64,3840]{1,0:T(8,128)(2,1)S(1)}, u32[]{:S(2)}, u32[]{:S(2)}) %collective-permute-start.22) | collective-permute-done | bytes 491552 | tf_op jit(solution)/shard_map/ppermute | solution.py:23
  451.5 1.9 convolution_convert_fusion
  453.6 13.8 %collective-permute-start.11 = (bf16[16,3584]{1,0:T(8,128)(2,1)S(1)}, bf16[16,3584]{1,0:T(8,128)(2,1)S(1)}, u32[]{:S(2)}, u32[]{:S(2)}) collective-permute-start(bf16[16,3584]{1,0:T(8,128)(2,1)S(1)} %fusion.153), channel_id=1, source_target_pairs={{8,0},{16,8},{24,16},{32,24},{40,32},{48,40},{56,48},{64,56},{72,6... | collective-permute-start | bytes 344072 | tf_op jit(solution)/shard_map/ppermute | solution.py:13
  467.8 1.9 fusion.7
  469.7 4.2 collective-permute-start.7
  473.9 2.2 fusion.199
  476.2 1.9 collective-permute-start.15
  478.2 0.7 maximum_bitcast_fusion
  478.9 8.3 %collective-permute-done.15 = bf16[16,3584]{1,0:T(8,128)(2,1)S(1)} collective-permute-done((bf16[16,3584]{1,0:T(8,128)(2,1)S(1)}, bf16[16,3584]{1,0:T(8,128)(2,1)S(1)}, u32[]{:S(2)}, u32[]{:S(2)}) %collective-permute-start.15) | collective-permute-done | bytes 114720 | tf_op jit(solution)/shard_map/ppermute | solution.py:13
  487.2 0.7 maximum_bitcast_fusion.1
  487.9 30.9 %reduce-scatter.2.cloned.1.call-done = bf16[448,256]{1,0:T(8,128)(2,1)} async-done(((bf16[3584,256]{1,0:T(8,128)(2,1)}), bf16[448,256]{1,0:T(8,128)(2,1)}) %reduce-scatter.2.cloned.1.call-update) | async-done | bytes 229392 | tf_op jit(solution)/shard_map/reduce_scatter | solution.py:168
  518.8 1.7 bitcast_convert_fusion
  (214 shorter events, 37.3 us)
Async XLA Ops:
  7.2 30.7 %copy-start.2 = (bf16[2,1,16,3584]{3,2,1,0:T(8,128)(2,1)S(1)}, bf16[2,1,16,3584]{3,2,1,0:T(8,128)(2,1)}, u32[]{:S(2)}) copy-start(bf16[2,1,16,3584]{3,2,1,0:T(8,128)(2,1)} %param.10) | copy-start | bytes 688132
  7.2 29.0 %copy-start.3 = (bf16[2,1,16,3584]{3,2,1,0:T(8,128)(2,1)S(1)}, bf16[2,1,16,3584]{3,2,1,0:T(8,128)(2,1)}, u32[]{:S(2)}) copy-start(bf16[2,1,16,3584]{3,2,1,0:T(8,128)(2,1)} %param.11) | copy-start | bytes 688132
  7.2 511.6 %reduce-scatter.2.cloned.1.call-start = ((), (), s32[]{:S(2)}) async-start(), calls=%async_computation.1 | async-start | bytes 2064384 | tf_op jit(solution)/shard_map/reduce_scatter | solution.py:168
  28.1 8.1 %copy-start = (bf16[1,2,256,3584]{3,2,1,0:T(8,128)(2,1)S(1)}, bf16[1,2,256,3584]{3,2,1,0:T(8,128)(2,1)}, u32[]{:S(2)}) copy-start(bf16[1,2,256,3584]{3,2,1,0:T(8,128)(2,1)} %param.14) | copy-start | bytes 11010052
  35.8 23.3 %copy-start.1 = (bf16[1,2,3584,256]{3,2,1,0:T(8,128)(2,1)S(1)}, bf16[1,2,3584,256]{3,2,1,0:T(8,128)(2,1)}, u32[]{:S(2)}) copy-start(bf16[1,2,3584,256]{3,2,1,0:T(8,128)(2,1)} %param.13) | copy-start | bytes 11010052
  38.2 35.7 %collective-permute-start.4 = (bf16[16,3584]{1,0:T(8,128)(2,1)S(1)}, bf16[16,3584]{1,0:T(8,128)(2,1)S(1)}, u32[]{:S(2)}, u32[]{:S(2)}) collective-permute-start(bf16[16,3584]{1,0:T(8,128)(2,1)S(1)} %fusion.4), channel_id=1, source_target_pairs={{8,0},{16,8},{24,16},{32,24},{40,32},{48,40},{56,48},{64,56},{72,6... | collective-permute-start | bytes 344072 | tf_op jit(solution)/shard_map/ppermute | solution.py:13
  61.4 12.7 %collective-permute-start = (bf16[16,3584]{1,0:T(8,128)(2,1)S(1)}, bf16[16,3584]{1,0:T(8,128)(2,1)S(1)}, u32[]{:S(2)}, u32[]{:S(2)}) collective-permute-start(bf16[16,3584]{1,0:T(8,128)(2,1)S(1)} %fusion), channel_id=1, source_target_pairs={{0,8},{8,16},{16,24},{24,32},{32,40},{40,48},{48,56},{56,64},{64,7... | collective-permute-start | bytes 344072 | tf_op jit(solution)/shard_map/ppermute | solution.py:13
  76.0 9.6 %collective-permute-start.8 = (bf16[16,3584]{1,0:T(8,128)(2,1)S(1)}, bf16[16,3584]{1,0:T(8,128)(2,1)S(1)}, u32[]{:S(2)}, u32[]{:S(2)}) collective-permute-start(bf16[16,3584]{1,0:T(8,128)(2,1)S(1)} %get-tuple-element.56), channel_id=1, source_target_pairs={{8,0},{16,8},{24,16},{32,24},{40,32},{48,40},{56,48},{64,56},{72,6... | collective-permute-start | bytes 344072 | tf_op jit(solution)/shard_map/ppermute | solution.py:13
  83.3 9.7 %collective-permute-start.12 = (bf16[16,3584]{1,0:T(8,128)(2,1)S(1)}, bf16[16,3584]{1,0:T(8,128)(2,1)S(1)}, u32[]{:S(2)}, u32[]{:S(2)}) collective-permute-start(bf16[16,3584]{1,0:T(8,128)(2,1)S(1)} %get-tuple-element.57), channel_id=1, source_target_pairs={{0,8},{8,16},{16,24},{24,32},{32,40},{40,48},{48,56},{56,64},{64,7... | collective-permute-start | bytes 344072 | tf_op jit(solution)/shard_map/ppermute | solution.py:13
  95.6 14.2 %collective-permute-start.1 = (bf16[16,3584]{1,0:T(8,128)(2,1)S(1)}, bf16[16,3584]{1,0:T(8,128)(2,1)S(1)}, u32[]{:S(2)}, u32[]{:S(2)}) collective-permute-start(bf16[16,3584]{1,0:T(8,128)(2,1)S(1)} %fusion.1), channel_id=1, source_target_pairs={{0,8},{8,16},{16,24},{24,32},{32,40},{40,48},{48,56},{56,64},{64,7... | collective-permute-start | bytes 344072 | tf_op jit(solution)/shard_map/ppermute | solution.py:13
  98.7 13.9 %collective-permute-start.5 = (bf16[16,3584]{1,0:T(8,128)(2,1)S(1)}, bf16[16,3584]{1,0:T(8,128)(2,1)S(1)}, u32[]{:S(2)}, u32[]{:S(2)}) collective-permute-start(bf16[16,3584]{1,0:T(8,128)(2,1)S(1)} %fusion.5), channel_id=1, source_target_pairs={{8,0},{16,8},{24,16},{32,24},{40,32},{48,40},{56,48},{64,56},{72,6... | collective-permute-start | bytes 344072 | tf_op jit(solution)/shard_map/ppermute | solution.py:13
  106.9 4.3 collective-permute-start.9
  113.9 22.2 %collective-permute-start.2 = (bf16[16,3584]{1,0:T(8,128)(2,1)S(1)}, bf16[16,3584]{1,0:T(8,128)(2,1)S(1)}, u32[]{:S(2)}, u32[]{:S(2)}) collective-permute-start(bf16[16,3584]{1,0:T(8,128)(2,1)S(1)} %fusion.2), channel_id=1, source_target_pairs={{0,8},{8,16},{16,24},{24,32},{32,40},{40,48},{48,56},{56,64},{64,7... | collective-permute-start | bytes 344072 | tf_op jit(solution)/shard_map/ppermute | solution.py:13
  117.0 43.3 %collective-permute-start.10 = (bf16[16,3584]{1,0:T(8,128)(2,1)S(1)}, bf16[16,3584]{1,0:T(8,128)(2,1)S(1)}, u32[]{:S(2)}, u32[]{:S(2)}) collective-permute-start(bf16[16,3584]{1,0:T(8,128)(2,1)S(1)} %fusion.151), channel_id=1, source_target_pairs={{8,0},{16,8},{24,16},{32,24},{40,32},{48,40},{56,48},{64,56},{72,6... | collective-permute-start | bytes 344072 | tf_op jit(solution)/shard_map/ppermute | solution.py:13
  125.0 9.7 %collective-permute-start.13 = (bf16[16,3584]{1,0:T(8,128)(2,1)S(1)}, bf16[16,3584]{1,0:T(8,128)(2,1)S(1)}, u32[]{:S(2)}, u32[]{:S(2)}) collective-permute-start(bf16[16,3584]{1,0:T(8,128)(2,1)S(1)} %get-tuple-element.63), channel_id=1, source_target_pairs={{0,8},{8,16},{16,24},{24,32},{32,40},{40,48},{48,56},{56,64},{64,7... | collective-permute-start | bytes 344072 | tf_op jit(solution)/shard_map/ppermute | solution.py:13
  137.4 4.3 collective-permute-start.6
  142.6 9.8 %collective-permute-start.14 = (bf16[16,3584]{1,0:T(8,128)(2,1)S(1)}, bf16[16,3584]{1,0:T(8,128)(2,1)S(1)}, u32[]{:S(2)}, u32[]{:S(2)}) collective-permute-start(bf16[16,3584]{1,0:T(8,128)(2,1)S(1)} %get-tuple-element.61), channel_id=1, source_target_pairs={{0,8},{8,16},{16,24},{24,32},{32,40},{40,48},{48,56},{56,64},{64,7... | collective-permute-start | bytes 344072 | tf_op jit(solution)/shard_map/ppermute | solution.py:13
  154.4 3.8 collective-permute-start.16
  158.1 15.1 %collective-permute-start.17 = (bf16[64,3840]{1,0:T(8,128)(2,1)S(1)}, bf16[64,3840]{1,0:T(8,128)(2,1)S(1)}, u32[]{:S(2)}, u32[]{:S(2)}) collective-permute-start(bf16[64,3840]{1,0:T(8,128)(2,1)S(1)} %collective-permute-done.16), channel_id=1, source_target_pairs={{0,16},{16,0},{8,24},{24,8},{32,48},{48,32},{40,56},{56,40},{64,80... | collective-permute-start | bytes 1474568 | tf_op jit(solution)/shard_map/ppermute | solution.py:23
  173.3 25.7 %collective-permute-start.18 = (bf16[64,3840]{1,0:T(8,128)(2,1)S(1)}, bf16[64,3840]{1,0:T(8,128)(2,1)S(1)}, u32[]{:S(2)}, u32[]{:S(2)}) collective-permute-start(bf16[64,3840]{1,0:T(8,128)(2,1)S(1)} %collective-permute-done.17), channel_id=1, source_target_pairs={{0,32},{32,0},{8,40},{40,8},{16,48},{48,16},{24,56},{56,24},{64,96... | collective-permute-start | bytes 1474568 | tf_op jit(solution)/shard_map/ppermute | solution.py:23
  199.0 49.2 %collective-permute-start.19 = (bf16[64,3840]{1,0:T(8,128)(2,1)S(1)}, bf16[64,3840]{1,0:T(8,128)(2,1)S(1)}, u32[]{:S(2)}, u32[]{:S(2)}) collective-permute-start(bf16[64,3840]{1,0:T(8,128)(2,1)S(1)} %collective-permute-done.18), channel_id=1, source_target_pairs={{0,64},{64,0},{8,72},{72,8},{16,80},{80,16},{24,88},{88,24},{32,96... | collective-permute-start | bytes 1474568 | tf_op jit(solution)/shard_map/ppermute | solution.py:23
  248.2 121.8 %collective-permute-start.20 = (bf16[64,3840]{1,0:T(8,128)(2,1)S(1)}, bf16[64,3840]{1,0:T(8,128)(2,1)S(1)}, u32[]{:S(2)}, u32[]{:S(2)}) collective-permute-start(bf16[64,3840]{1,0:T(8,128)(2,1)S(1)} %collective-permute-done.19), channel_id=1, source_target_pairs={{0,128},{128,0},{8,136},{136,8},{16,144},{144,16},{24,152},{152,24... | collective-permute-start | bytes 1474568 | tf_op jit(solution)/shard_map/ppermute | solution.py:23
  370.0 47.0 %collective-permute-start.21 = (bf16[64,3840]{1,0:T(8,128)(2,1)S(1)}, bf16[64,3840]{1,0:T(8,128)(2,1)S(1)}, u32[]{:S(2)}, u32[]{:S(2)}) collective-permute-start(bf16[64,3840]{1,0:T(8,128)(2,1)S(1)} %collective-permute-done.20), channel_id=1, source_target_pairs={{0,256},{256,0},{8,264},{264,8},{16,272},{272,16},{24,280},{280,24... | collective-permute-start | bytes 1474568 | tf_op jit(solution)/shard_map/ppermute | solution.py:23
  372.3 105.9 %collective-permute-start.3 = (bf16[16,3584]{1,0:T(8,128)(2,1)S(1)}, bf16[16,3584]{1,0:T(8,128)(2,1)S(1)}, u32[]{:S(2)}, u32[]{:S(2)}) collective-permute-start(bf16[16,3584]{1,0:T(8,128)(2,1)S(1)} %fusion.3), channel_id=1, source_target_pairs={{0,8},{8,16},{16,24},{24,32},{32,40},{40,48},{48,56},{56,64},{64,7... | collective-permute-start | bytes 344072 | tf_op jit(solution)/shard_map/ppermute | solution.py:13
  417.1 34.4 %collective-permute-start.22 = (bf16[64,3840]{1,0:T(8,128)(2,1)S(1)}, bf16[64,3840]{1,0:T(8,128)(2,1)S(1)}, u32[]{:S(2)}, u32[]{:S(2)}) collective-permute-start(bf16[64,3840]{1,0:T(8,128)(2,1)S(1)} %collective-permute-done.21), channel_id=1, source_target_pairs={{0,512},{512,0},{8,520},{520,8},{16,528},{528,16},{24,536},{536,24... | collective-permute-start | bytes 1474568 | tf_op jit(solution)/shard_map/ppermute | solution.py:23
  453.6 25.3 %collective-permute-start.11 = (bf16[16,3584]{1,0:T(8,128)(2,1)S(1)}, bf16[16,3584]{1,0:T(8,128)(2,1)S(1)}, u32[]{:S(2)}, u32[]{:S(2)}) collective-permute-start(bf16[16,3584]{1,0:T(8,128)(2,1)S(1)} %fusion.153), channel_id=1, source_target_pairs={{8,0},{16,8},{24,16},{32,24},{40,32},{48,40},{56,48},{64,56},{72,6... | collective-permute-start | bytes 344072 | tf_op jit(solution)/shard_map/ppermute | solution.py:13
  469.7 8.5 %collective-permute-start.7 = (bf16[16,3584]{1,0:T(8,128)(2,1)S(1)}, bf16[16,3584]{1,0:T(8,128)(2,1)S(1)}, u32[]{:S(2)}, u32[]{:S(2)}) collective-permute-start(bf16[16,3584]{1,0:T(8,128)(2,1)S(1)} %fusion.7), channel_id=1, source_target_pairs={{8,0},{16,8},{24,16},{32,24},{40,32},{48,40},{56,48},{64,56},{72,6... | collective-permute-start | bytes 344072 | tf_op jit(solution)/shard_map/ppermute | solution.py:13
  476.2 11.0 %collective-permute-start.15 = (bf16[16,3584]{1,0:T(8,128)(2,1)S(1)}, bf16[16,3584]{1,0:T(8,128)(2,1)S(1)}, u32[]{:S(2)}, u32[]{:S(2)}) collective-permute-start(bf16[16,3584]{1,0:T(8,128)(2,1)S(1)} %fusion.161), channel_id=1, source_target_pairs={{0,8},{8,16},{16,24},{24,32},{32,40},{40,48},{48,56},{56,64},{64,7... | collective-permute-start | bytes 344072 | tf_op jit(solution)/shard_map/ppermute | solution.py:13
Sparse Core Ops, SparseCore 0:
  453.5 65.1 reduce-scatter.1
where the time goes:
time: 533 us; the launch traced here: 527 us
  waiting for transfers between devices  317 us (59%)
  starting transfers between devices  114 us (21%)
  matrix products  37.5 us (7%)
  between operations  30.6 us (6%)
  other arithmetic  21 us (4%)
  local copies, waits for them, and re-layouts  7.24 us (1%)
    ppermute x7, waiting for transfers between devices, swapped(): return lax.ppermute(block, axis, route)  255 us
    ppermute x16, starting transfers between devices, passed_along(): return lax.ppermute(shard, axis, pairs)  78 us
    ppermute x7, starting transfers between devices, swapped(): return lax.ppermute(block, axis, route)  35.9 us
    ppermute x16, waiting for transfers between devices, passed_along(): return lax.ppermute(shard, axis, pairs)  31.1 us
    reduce_scatter x1, waiting for transfers between devices, shards(): lax.psum_scatter(lax.optimization_barrier(partial_value.astype(jnp.bfloat...  30.9 us
    dot_general x16, matrix products, contract_last(): lax.dot_general(left, right, (((1,), (1,)), ((), ())), preferred_element_...  11.6 us
  transfers between devices with their start and end apart: 24, of which 15 were waited for; matrix products, arithmetic and copies ran while one was open for 8% of the time, Pallas kernels for 0%

commit v1 on v0

v1 whole, which is shorter than its diff:
```python
import functools

import jax
import jax.numpy as jnp
from jax import lax
from jax.experimental import pallas as pl
from jax.experimental.pallas import tpu as pltpu
from jax.sharding import PartitionSpec as P

epsilon = 1e-06
score_factor = 2.0
vmem_limit = 12 * 1024 * 1024


def with_chip_partner(block):
    count = lax.axis_size("pipe")
    return lax.ppermute(block, "pipe", [(i, i ^ 1) for i in range(count)])


def with_outer_partner(block):
    count = lax.axis_size("pipe")
    pairs = []
    for low in range(1, count - 1, 2):
        pairs += [(low, low + 1), (low + 1, low)]
    return lax.ppermute(block, "pipe", pairs)


def from_mirror(block):
    count = lax.axis_size("pipe")
    return lax.ppermute(block, "pipe", [(i, count - 1 - i) for i in range(count)])


def contract(left, right, left_dim, right_dim):
    return lax.dot_general(
        left, right, (((left_dim,), (right_dim,)), ((), ())), preferred_element_type=jnp.float32
    )


def inverse_rms(values):
    return lax.rsqrt(jnp.mean(values * values, axis=-1, keepdims=True) + epsilon)


def probabilities_of(query_rows, key_rows, length):
    row_count, width = query_rows.shape
    scores = contract(query_rows, key_rows, 1, 1) * (score_factor / width)
    query_at = lax.broadcasted_iota(jnp.int32, (row_count, row_count), 0)
    key_at = lax.broadcasted_iota(jnp.int32, (row_count, row_count), 1)
    visible = (key_at <= query_at) & (key_at < length)
    weights = jnp.where(visible, jnp.exp(scores), 0.0)
    return weights / jnp.sum(weights, axis=-1, keepdims=True)


def prepare_kernel(
    place,
    forward_lengths,
    plan,
    stored_lengths,
    stored,
    forward_state,
    backward_state,
    w_down,
    gain,
    latent_gain,
    scalars_out,
    normed_out,
    to_mirror_out,
    inner_out,
    outer_out,
    grads_zero_out,
    grads_one_out,
    key_out,
    query_out,
    unit_out,
    latent_inverse_out,
    input_inverse_out,
    probabilities_out,
    weights,
    stored_here,
    gain_here,
    latent_gain_here,
    forward_lengths_here,
    plan_here,
    stored_lengths_here,
    weights_arrived,
    inputs_arrived,
    states_arrived,
    numbers_arrived,
    *,
    forward_lengths_at,
    plan_at,
):
    sides, slots, row_count = probabilities_out.shape[:3]
    replicas, block, columns = normed_out.shape
    steps = plan.shape[2]
    core = place[0]
    copies = [
        pltpu.make_async_copy(w_down.at[side], weights.at[side], weights_arrived.at[side])
        for side in range(sides)
    ]
    inputs = [
        pltpu.make_async_copy(source, target, inputs_arrived.at[at])
        for at, (source, target) in enumerate(
            ((gain, gain_here), (stored, stored_here), (latent_gain, latent_gain_here))
        )
    ]
    others = [
        pltpu.make_async_copy(source, target, numbers_arrived.at[at])
        for at, (source, target) in enumerate(
            (
                (forward_lengths, forward_lengths_here),
                (plan, plan_here),
                (stored_lengths, stored_lengths_here),
            )
        )
    ]
    others += [
        pltpu.make_async_copy(source.at[side], target, states_arrived.at[at])
        for at, (source, side, target) in enumerate(
            (
                (forward_state, 1 - core, inner_out.at[0:row_count]),
                (backward_state, core, inner_out.at[row_count : 2 * row_count]),
                (forward_state, core, outer_out.at[0:row_count]),
                (backward_state, 1 - core, outer_out.at[row_count : 2 * row_count]),
            )
        )
    ]
    for copy in inputs + copies + others:
        copy.start()
    grads_zero_out[...] = jnp.zeros(grads_zero_out.shape, grads_zero_out.dtype)
    grads_one_out[...] = jnp.zeros(grads_one_out.shape, grads_one_out.dtype)
    for copy in inputs:
        copy.wait()
    all_normed = []
    for side in range(sides):
        rows = stored_here[side].astype(jnp.float32)
        inverse = inverse_rms(rows)
        input_inverse_out[side] = jnp.broadcast_to(inverse, input_inverse_out.shape[1:])
        normed = (rows * inverse * gain_here[side : side + 1]).astype(jnp.bfloat16)
        all_normed.append(normed)
        for replica in range(replicas):
            part = normed[:, replica * columns : (replica + 1) * columns]
            (normed_out, to_mirror_out)[side][replica] = part
    for copy in others:
        copy.wait()
    scalars_out[0] = core
    for side in range(sides):
        for step in range(steps):
            scalars_out[forward_lengths_at + side * steps + step] = forward_lengths_here[
                side, 0, 0, step
            ]
            scalars_out[plan_at + side * steps + step] = plan_here[side, 0, step]
    for side in range(sides):
        copies[side].wait()
        latent = jnp.dot(all_normed[side], weights[side], preferred_element_type=jnp.float32)
        inverse = inverse_rms(latent)
        unit = latent * inverse
        key_rows = (unit * latent_gain_here[side, 0:1]).astype(jnp.bfloat16)
        query_rows = (unit * latent_gain_here[side, 1:2]).astype(jnp.bfloat16)
        latent_inverse_out[side] = jnp.broadcast_to(inverse, latent_inverse_out.shape[1:])
        unit_out[side] = unit
        key_out[side] = key_rows
        query_out[side] = query_rows
        for slot in range(slots):
            part = slice(slot * row_count, (slot + 1) * row_count)
            probabilities_out[side, slot] = probabilities_of(
                query_rows[part], key_rows[part], stored_lengths_here[side, 0, 0, slot]
            )


def normed_rows(rows, gain_row):
    return (rows * inverse_rms(rows) * gain_row).astype(jnp.bfloat16)


def forward_ended(rows, latent, side, length, w_up, latent_gain):
    unit = latent * inverse_rms(latent)
    gains = latent_gain[side]
    key_rows = (unit * gains[0:1]).astype(jnp.bfloat16)
    query_rows = (unit * gains[1:2]).astype(jnp.bfloat16)
    weights = probabilities_of(query_rows, key_rows, length).astype(jnp.bfloat16)
    mixed_rows = jnp.dot(weights, key_rows, preferred_element_type=jnp.float32)
    update = jnp.dot(
        mixed_rows.astype(jnp.bfloat16), w_up[side], preferred_element_type=jnp.float32
    )
    return (rows + update).astype(jnp.bfloat16)


def grad_latent_of(grad_mixed, side, slot, latent_gain, kept):
    keys, queries, units, latent_inverses, _, probabilities = kept
    row_count = grad_mixed.shape[0]
    mine = pl.ds(pl.multiple_of(slot * row_count, row_count), row_count)
    key_rows = keys[side, mine]
    query_rows = queries[side, mine]
    weights = probabilities[side, slot]
    gains = latent_gain[side]
    grad_mixed = grad_mixed.astype(jnp.bfloat16)
    grad_weights = contract(grad_mixed, key_rows, 1, 1)
    grad_scores = weights * (
        grad_weights - jnp.sum(grad_weights * weights, axis=-1, keepdims=True)
    )
    grad_scores = (grad_scores * (score_factor / key_rows.shape[1])).astype(jnp.bfloat16)
    grad_query = contract(grad_scores, key_rows, 1, 0)
    grad_key = contract(weights.astype(jnp.bfloat16), grad_mixed, 0, 0) + contract(
        grad_scores, query_rows, 0, 0
    )
    grad_unit = grad_key * gains[0:1] + grad_query * gains[1:2]
    unit = units[side, mine]
    return (
        latent_inverses[side, mine][:, 0:1]
        * (grad_unit - unit * jnp.mean(grad_unit * unit, axis=-1, keepdims=True))
    ).astype(jnp.bfloat16)


def backward_ended(grad_out, grad_latent, side, slot, stored, w_down, gain, kept):
    row_count = grad_out.shape[0]
    mine = pl.ds(pl.multiple_of(slot * row_count, row_count), row_count)
    grad_normed = contract(grad_latent, w_down[side], 1, 1)
    inverse = kept[4][side, mine][:, 0:1]
    unit = stored[side, mine].astype(jnp.float32) * inverse
    grad_unit = grad_normed * gain[pl.ds(side, 1)]
    grad_rows = inverse * (grad_unit - unit * jnp.mean(grad_unit * unit, axis=-1, keepdims=True))
    return (grad_out.astype(jnp.float32) + grad_rows).astype(jnp.bfloat16)


def of_slot(grad_latent, slot, slots):
    grad_latent = grad_latent.astype(jnp.float32)
    return jnp.concatenate(
        [jnp.where(slot == at, grad_latent, 0.0) for at in range(slots)], axis=0
    )


def half_step_kernel(
    scalars,
    arrived,
    stored,
    w_down,
    w_up,
    gain,
    latent_gain,
    *refs,
    forward_lane,
    lengths_at,
    plan_at,
    steps,
    step,
):
    kept, (grads_in, outgoing, grads_out) = refs[:6], refs[6:]
    row_count = outgoing.shape[0] // 2
    core = scalars[0]
    forward_side = forward_lane ^ core
    backward_side = 1 - forward_side
    slot = scalars[plan_at + backward_side * steps + step]
    length = scalars[lengths_at + forward_side * steps + step]
    rows = arrived[0:row_count].astype(jnp.float32)
    grad_out = arrived[row_count:]

    grad_mixed = contract(grad_out, w_up[backward_side], 1, 1)
    normed = normed_rows(rows, gain[pl.ds(forward_side, 1)])
    latent = jnp.dot(normed, w_down[forward_side], preferred_element_type=jnp.float32)
    grad_latent = grad_latent_of(grad_mixed, backward_side, slot, latent_gain, kept)
    grads_out[...] = grads_in[...] + of_slot(grad_latent, slot, grads_out.shape[0] // row_count)
    outgoing[0:row_count] = forward_ended(rows, latent, forward_side, length, w_up, latent_gain)
    outgoing[row_count:] = backward_ended(
        grad_out, grad_latent, backward_side, slot, stored, w_down, gain, kept
    )


def own_grads_kernel(place, grads_zero, grads_one, lower, upper):
    first = place[0] == 0
    lower[...] = jnp.where(first, grads_zero[...], grads_one[...]).astype(lower.dtype)
    upper[...] = jnp.where(first, grads_one[...], grads_zero[...]).astype(upper.dtype)


def own_states_kernel(place, inner, outer, forward_out, backward_out):
    core = place[0]
    row_count = forward_out.shape[1]
    forward_out[core] = outer[0:row_count]
    forward_out[1 - core] = inner[0:row_count]
    backward_out[core] = inner[row_count:]
    backward_out[1 - core] = outer[row_count:]


def pack_kernel(rows_lower, rows_upper, grads_lower, grads_upper, packed):
    replicas, block, columns = rows_lower.shape
    for replica in range(replicas):
        packed[replica, 0:block] = jnp.concatenate([rows_lower[replica], grads_lower[...]], axis=1)
        packed[replica, block:] = jnp.concatenate([rows_upper[replica], grads_upper[...]], axis=1)


def product_kernel(packed, result):
    replicas, block, width = packed.shape
    columns = result.shape[0]
    packed = packed[...].reshape(replicas * block, width)
    result[...] = contract(packed[:, :columns], packed[:, columns:], 0, 0)


def in_vmem(count):
    return [pl.BlockSpec(memory_space=pltpu.VMEM)] * count


def in_smem(count):
    return [pl.BlockSpec(memory_space=pltpu.SMEM)] * count


def like(*shape, dtype=jnp.float32):
    return jax.ShapeDtypeStruct(shape, dtype)


def call_kernel(kernel, outs, scalars, *operands, scalar_outs=0, in_hbm=(), scratch=(), aliases=()):
    specs = in_smem(len(scalars)) + in_vmem(len(operands))
    operands = list(operands)
    for at in in_hbm:
        specs[len(scalars) + at] = pl.BlockSpec(memory_space=pltpu.HBM)
        operands[at] = pltpu.with_memory_space_constraint(operands[at], pltpu.HBM)
    return pl.pallas_call(
        kernel,
        out_shape=outs,
        in_specs=specs,
        out_specs=in_smem(scalar_outs) + in_vmem(len(outs) - scalar_outs),
        scratch_shapes=scratch,
        input_output_aliases={len(scalars) + taken: given for taken, given in aliases},
        compiler_params=pltpu.CompilerParams(vmem_limit_bytes=vmem_limit),
        cost_estimate=pl.CostEstimate(flops=1000000, bytes_accessed=1000, transcendentals=0),
    )(*scalars, *operands)


def shards(
    forward_state,
    backward_state,
    stored_inputs,
    down_weight,
    up_weight,
    norm_gain,
    latent_gain,
    forward_lengths,
    stored_lengths,
    plan,
):
    sides = stored_inputs.shape[0]
    slot_count, row_count, features = stored_inputs.shape[2:]
    latent_width = down_weight.shape[3]
    tick_count = forward_lengths.shape[2]
    replicas = lax.axis_size("dp")
    columns = features // replicas
    block = slot_count * row_count
    forward_lengths_at = 1
    plan_at = forward_lengths_at + sides * tick_count
    narrow = jnp.bfloat16

    place = (lax.axis_index("pipe") % 2).astype(jnp.int32).reshape(1)

    stored = stored_inputs.reshape(sides, block, features)
    w_down = down_weight[0]
    w_up = up_weight[0]
    gain = norm_gain[0]
    gains_latent = latent_gain[0]

    numbers = (
        jnp.transpose(forward_lengths, (0, 1, 3, 2)),
        plan,
        jnp.transpose(stored_lengths, (0, 1, 3, 2)),
    )

    scalars, normed, to_mirror, *carry = call_kernel(
        functools.partial(prepare_kernel, forward_lengths_at=forward_lengths_at, plan_at=plan_at),
        [
            like(plan_at + sides * tick_count, dtype=jnp.int32),
            like(replicas, block, columns, dtype=narrow),
            like(replicas, block, columns, dtype=narrow),
            like(2 * row_count, features, dtype=narrow),
            like(2 * row_count, features, dtype=narrow),
            like(block, latent_width),
            like(block, latent_width),
            like(sides, block, latent_width, dtype=narrow),
            like(sides, block, latent_width, dtype=narrow),
            like(sides, block, latent_width),
            like(sides, block, 128),
            like(sides, block, 128),
            like(sides, slot_count, row_count, row_count),
        ],
        [place],
        numbers[0],
        numbers[1],
        numbers[2],
        stored,
        forward_state[:, 0],
        backward_state[:, 0],
        w_down,
        gain,
        gains_latent,
        scalar_outs=1,
        in_hbm=range(9),
        scratch=[
            pltpu.VMEM((sides, features, latent_width), narrow),
            pltpu.VMEM(stored.shape, stored.dtype),
            pltpu.VMEM(gain.shape, gain.dtype),
            pltpu.VMEM(gains_latent.shape, gains_latent.dtype),
            *[pltpu.SMEM(array.shape, jnp.int32) for array in numbers],
            pltpu.SemaphoreType.DMA((sides,)),
            pltpu.SemaphoreType.DMA((3,)),
            pltpu.SemaphoreType.DMA((4,)),
            pltpu.SemaphoreType.DMA((3,)),
        ],
    )

    carry, kept = carry[:4], carry[4:]

    def half_step(forward_lane, step, arrived, grads):
        return call_kernel(
            functools.partial(
                half_step_kernel,
                forward_lane=forward_lane,
                lengths_at=forward_lengths_at,
                plan_at=plan_at,
                steps=tick_count,
                step=step,
            ),
            [like(2 * row_count, features, dtype=narrow), like(block, latent_width)],
            [scalars],
            arrived,
            stored,
            w_down,
            w_up,
            gain,
            gains_latent,
            *kept,
            grads,
            aliases=((12, 1),),
        )

    inner, outer, grads_zero, grads_one = carry
    for step in range(tick_count):
        if step == tick_count - 1:
            outer, to_mirror = lax.optimization_barrier((outer, to_mirror))
        to_outer, grads_zero = half_step(1, step, inner, grads_zero)
        to_inner, grads_one = half_step(0, step, outer, grads_one)
        inner = with_chip_partner(to_inner)
        outer = with_outer_partner(to_outer)

    mirrored = from_mirror(to_mirror)
    sums_lower, sums_upper = call_kernel(
        own_grads_kernel,
        [like(block, latent_width, dtype=narrow)] * 2,
        [place],
        grads_zero,
        grads_one,
    )
    sums_mirrored = from_mirror(sums_upper)
    mirrored, sums_mirrored, inner, outer = lax.optimization_barrier(
        (mirrored, sums_mirrored, inner, outer)
    )
    (packed,) = call_kernel(
        pack_kernel,
        [like(replicas, 2 * block, columns + latent_width, dtype=narrow)],
        [],
        normed,
        mirrored,
        sums_lower,
        sums_mirrored,
    )
    packed = lax.all_to_all(packed, "dp", split_axis=0, concat_axis=0, tiled=True)
    (grad_down,) = call_kernel(product_kernel, [like(columns, latent_width)], [], packed)
    forward_out, backward_out = call_kernel(
        own_states_kernel,
        [like(2, row_count, features, dtype=narrow)] * 2,
        [place],
        inner,
        outer,
    )
    return (forward_out[:, None], backward_out[:, None], grad_down[None])


def solution(mesh):
    in_specs = (
        P(None, "pipe", "dp", None),
        P(None, "pipe", "dp", None),
        P(None, "pipe", None, "dp", None),
        P("pipe", None, None, None),
        P("pipe", None, None, None),
        P("pipe", None, None),
        P("pipe", None, None, None),
        P(None, "pipe", None, "dp"),
        P(None, "pipe", None, "dp"),
        P(None, "pipe", None),
    )
    out_specs = (P(None, "pipe", "dp", None), P(None, "pipe", "dp", None), P("pipe", "dp", None))
    return jax.shard_map(shards, mesh=mesh, in_specs=in_specs, out_specs=out_specs, check_vma=False)
```

time: 533 us -> 144 us (0.27)
  waiting for transfers between devices: 317 us -> 53.3 us
  starting transfers between devices: 114 us -> 54.8 us
  matrix products: 37.5 us -> 0 us
  Pallas kernels: 0 us -> 32.2 us
  between operations: 30.6 us -> 0.92 us
  other arithmetic: 21 us -> 0 us
    ppermute x23 -> x10, waiting for transfers between devices: 286 us -> 44.2 us  [the longest x2 42.1 us: from_mirror(): lax.ppermute(block, 'pipe', [(i, count - 1 - i) for i in range(count)])]
    ppermute x23 -> x10, starting transfers between devices: 114 us -> 49.1 us  [the longest x4 31.7 us: with_outer_partner(): return lax.ppermute(block, 'pipe', pairs)]
    dot_general x89 -> x0, matrix products: 37.5 us -> none  [the longest x16 11.6 us: contract_last(): lax.dot_general(left, right, (((1,), (1,)), ((), ())), preferred_element_...]
    pallas_call x0 -> x13, Pallas kernels: none -> 32.2 us  [call_kernel(): pl.pallas_call(kernel, out_shape=outs, in_specs=specs, out_specs=in_smem(...]
    reduce_scatter x1 -> x0, waiting for transfers between devices: 30.9 us -> none  [shards(): lax.psum_scatter(lax.optimization_barrier(partial_value.astype(jnp.bfloat...]
    lt x16 -> x0, other arithmetic: 10.5 us -> none  [attend(): position[None, None, :] < length[:, None, None]]
    all_to_all x0 -> x1, waiting for transfers between devices: none -> 9.02 us  [shards(): lax.all_to_all(packed, 'dp', split_axis=0, concat_axis=0, tiled=True)]
    slice x6 -> x0, local copies, waits for them, and re-layouts: 6.47 us -> none  [the longest x1 1.53 us: run_side(): slot_index = plan[side_index, 0, step_index]]
  transfers between devices with their start and end apart: 24 -> 11, of which waited for: 15 -> 3; matrix products, arithmetic and copies ran while one was open for 8% -> 0% of each run, Pallas kernels for 0% -> 16%
where the time goes in v1:
time: 144 us; the launch traced here: 143 us
  starting transfers between devices  54.8 us (38%)
  waiting for transfers between devices  53.3 us (37%)
  Pallas kernels  32.2 us (22%)
  local copies, waits for them, and re-layouts  2.05 us (1%)
    ppermute x2, waiting for transfers between devices, from_mirror(): lax.ppermute(block, 'pipe', [(i, count - 1 - i) for i in range(count)])  42.1 us
    pallas_call x13, Pallas kernels, call_kernel(): pl.pallas_call(kernel, out_shape=outs, in_specs=specs, out_specs=in_smem(...  32.2 us
    ppermute x4, starting transfers between devices, with_outer_partner(): return lax.ppermute(block, 'pipe', pairs)  31.7 us
    ppermute x2, starting transfers between devices, from_mirror(): lax.ppermute(block, 'pipe', [(i, count - 1 - i) for i in range(count)])  9.18 us
    all_to_all x1, waiting for transfers between devices, shards(): lax.all_to_all(packed, 'dp', split_axis=0, concat_axis=0, tiled=True)  9.02 us
    ppermute x4, starting transfers between devices, with_chip_partner(): return lax.ppermute(block, 'pipe', [(i, i ^ 1) for i in range(count)])  8.17 us
    all_to_all x1, starting transfers between devices, shards(): lax.all_to_all(packed, 'dp', split_axis=0, concat_axis=0, tiled=True)  5.76 us
  transfers between devices with their start and end apart: 11, of which 3 were waited for; matrix products, arithmetic and copies ran while one was open for 0% of the time, Pallas kernels for 16%

profile of v1, /device:TPU:24, one launch (start us, length us, event | category | flops | bytes accessed | tf_op | source)
XLA Modules:
  0.0 143.3 jit_solution(8716455569666774515)
XLA Ops:
  0.6 0.0 copy-start.4
  0.6 0.0 copy-start.3
  0.7 0.0 copy-start.2
  0.7 0.0 copy-start
  0.7 4.4 %shard_map.121 = (s32[17]{0:T(128)S(1)}, bf16[8,32,448]{2,1,0:T(8,128)(2,1)S(1)}, bf16[8,32,448]{2,1,0:T(8,128)(2,1)S(1)}, bf16[32,3584]{1,0:T(8,128)(2,1)S(1)},...) custom-call(s32[1]{0:T(128)} %bitcast.place, ...), custom_call_target="tpu_custom_call" | custom-call | flops 1000000 | bytes 1000 | tf_op jit(solution)/shard_map/pallas_call | solution.py:314
  5.1 0.0 copy-done.4
  5.1 0.0 copy-done.3
  5.1 0.0 copy-done.2
  5.1 0.0 copy-done
  5.1 0.0 copy-start.1
  5.1 2.0 %copy-done.1 = bf16[1,2,256,3584]{3,2,1,0:T(8,128)(2,1)S(1)} copy-done((bf16[1,2,256,3584]{3,2,1,0:T(8,128)(2,1)S(1)}, bf16[1,2,256,3584]{3,2,1,0:T(8,128)(2,1)}, u32[]{:S(2)}) %copy-start.1) | copy-done | bytes 3670040
  7.1 3.1 %shard_map.122 = (bf16[32,3584]{1,0:T(8,128)(2,1)S(1)}, f32[32,256]{1,0:T(8,128)S(1)}) custom-call(s32[17]{0:T(128)S(1)} %get-tuple-element.42.scalars, bf16[32,3584]{1,0:T(8,128)(2,1)S(1)} %get-tuple-element.43.arrived, bf16[2,32,3584]{2,1,0:T(8,128)(2,1)S(1)} %bitcast.39, bf16[2,3584,256]{2,1,0:T(8,128)(2,1)S(1)} %bitcast.22, ...), custom_call_target="tpu_custom_call", output_to_operand_aliasing={{1}: (13, {})} | custom-call | flops 1000000 | bytes 1000 | tf_op jit(solution)/shard_map/pallas_call | solution.py:314
  10.2 18.8 %collective-permute-start = (bf16[32,3584]{1,0:T(8,128)(2,1)S(1)}, bf16[32,3584]{1,0:T(8,128)(2,1)S(1)}, u32[]{:S(2)}, u32[]{:S(2)}) collective-permute-start(bf16[32,3584]{1,0:T(8,128)(2,1)S(1)} %get-tuple-element.51), channel_id=1, source_target_pairs={{8,16},{16,8},{24,32},{32,24},{40,48},{48,40},{56,64},{64,56},{72,... | collective-permute-start | bytes 688136 | tf_op jit(solution)/shard_map/ppermute | solution.py:25
  29.0 3.1 %shard_map.123 = (bf16[32,3584]{1,0:T(8,128)(2,1)S(1)}, f32[32,256]{1,0:T(8,128)S(1)}) custom-call(s32[17]{0:T(128)S(1)} %get-tuple-element.42.scalars, bf16[32,3584]{1,0:T(8,128)(2,1)S(1)} %get-tuple-element.52.arrived, bf16[2,32,3584]{2,1,0:T(8,128)(2,1)S(1)} %bitcast.40, bf16[2,3584,256]{2,1,0:T(8,128)(2,1)S(1)} %bitcast.23, ...), custom_call_target="tpu_custom_call", output_to_operand_aliasing={{1}: (13, {})} | custom-call | flops 1000000 | bytes 1000 | tf_op jit(solution)/shard_map/pallas_call | solution.py:314
  32.1 1.9 %collective-permute-start.2 = (bf16[32,3584]{1,0:T(8,128)(2,1)S(1)}, bf16[32,3584]{1,0:T(8,128)(2,1)S(1)}, u32[]{:S(2)}, u32[]{:S(2)}) collective-permute-start(bf16[32,3584]{1,0:T(8,128)(2,1)S(1)} %get-tuple-element.56), channel_id=1, source_target_pairs={{0,8},{8,0},{16,24},{24,16},{32,40},{40,32},{48,56},{56,48},{64,72... | collective-permute-start | bytes 688136 | tf_op jit(solution)/shard_map/ppermute | solution.py:17
  34.1 0.0 collective-permute-done.arrived
  34.1 3.1 %shard_map.124 = (bf16[32,3584]{1,0:T(8,128)(2,1)S(1)}, f32[32,256]{1,0:T(8,128)S(1)}) custom-call(s32[17]{0:T(128)S(1)} %get-tuple-element.42.scalars, bf16[32,3584]{1,0:T(8,128)(2,1)S(1)} %collective-permute-done.arrived, bf16[2,32,3584]{2,1,0:T(8,128)(2,1)S(1)} %bitcast.41, bf16[2,3584,256]{2,1,0:T(8,128)(2,1)S(1)} %bitcast.24, ...), custom_call_target="tpu_custom_call", output_to_operand_aliasing={{1}: (13, {})} | custom-call | flops 1000000 | bytes 1000 | tf_op jit(solution)/shard_map/pallas_call | solution.py:314
  37.2 2.4 %collective-permute-start.1 = (bf16[32,3584]{1,0:T(8,128)(2,1)S(1)}, bf16[32,3584]{1,0:T(8,128)(2,1)S(1)}, u32[]{:S(2)}, u32[]{:S(2)}) collective-permute-start(bf16[32,3584]{1,0:T(8,128)(2,1)S(1)} %get-tuple-element.55), channel_id=1, source_target_pairs={{0,8},{8,0},{16,24},{24,16},{32,40},{40,32},{48,56},{56,48},{64,72... | collective-permute-start | bytes 688136 | tf_op jit(solution)/shard_map/ppermute | solution.py:17
  39.6 0.0 collective-permute-done.2.arrived
  39.6 3.1 %shard_map.125 = (bf16[32,3584]{1,0:T(8,128)(2,1)S(1)}, f32[32,256]{1,0:T(8,128)S(1)}) custom-call(s32[17]{0:T(128)S(1)} %get-tuple-element.42.scalars, bf16[32,3584]{1,0:T(8,128)(2,1)S(1)} %collective-permute-done.2.arrived, bf16[2,32,3584]{2,1,0:T(8,128)(2,1)S(1)} %bitcast.42, ...), custom_call_target="tpu_custom_call", output_to_operand_aliasing={{1}: (13, {})} | custom-call | flops 1000000 | bytes 1000 | tf_op jit(solution)/shard_map/pallas_call | solution.py:314
  42.7 5.4 %collective-permute-start.5 = (bf16[32,3584]{1,0:T(8,128)(2,1)S(1)}, bf16[32,3584]{1,0:T(8,128)(2,1)S(1)}, u32[]{:S(2)}, u32[]{:S(2)}) collective-permute-start(bf16[32,3584]{1,0:T(8,128)(2,1)S(1)} %get-tuple-element.62), channel_id=1, source_target_pairs={{8,16},{16,8},{24,32},{32,24},{40,48},{48,40},{56,64},{64,56},{72,... | collective-permute-start | bytes 688136 | tf_op jit(solution)/shard_map/ppermute | solution.py:25
  48.1 0.0 collective-permute-done.1.arrived
  48.1 3.1 %shard_map.126 = (bf16[32,3584]{1,0:T(8,128)(2,1)S(1)}, f32[32,256]{1,0:T(8,128)S(1)}) custom-call(s32[17]{0:T(128)S(1)} %get-tuple-element.42.scalars, bf16[32,3584]{1,0:T(8,128)(2,1)S(1)} %collective-permute-done.1.arrived, bf16[2,32,3584]{2,1,0:T(8,128)(2,1)S(1)} %bitcast.43, ...), custom_call_target="tpu_custom_call", output_to_operand_aliasing={{1}: (13, {})} | custom-call | flops 1000000 | bytes 1000 | tf_op jit(solution)/shard_map/pallas_call | solution.py:314
  51.3 3.8 %collective-permute-start.3 = (bf16[32,3584]{1,0:T(8,128)(2,1)S(1)}, bf16[32,3584]{1,0:T(8,128)(2,1)S(1)}, u32[]{:S(2)}, u32[]{:S(2)}) collective-permute-start(bf16[32,3584]{1,0:T(8,128)(2,1)S(1)} %get-tuple-element.59), channel_id=1, source_target_pairs={{8,16},{16,8},{24,32},{32,24},{40,48},{48,40},{56,64},{64,56},{72,... | collective-permute-start | bytes 688136 | tf_op jit(solution)/shard_map/ppermute | solution.py:25
  55.0 0.0 collective-permute-done.5.arrived
  55.0 3.1 %shard_map.127 = (bf16[32,3584]{1,0:T(8,128)(2,1)S(1)}, f32[32,256]{1,0:T(8,128)S(1)}) custom-call(s32[17]{0:T(128)S(1)} %get-tuple-element.42.scalars, bf16[32,3584]{1,0:T(8,128)(2,1)S(1)} %collective-permute-done.5.arrived, bf16[2,32,3584]{2,1,0:T(8,128)(2,1)S(1)} %bitcast.44, ...), custom_call_target="tpu_custom_call", output_to_operand_aliasing={{1}: (13, {})} | custom-call | flops 1000000 | bytes 1000 | tf_op jit(solution)/shard_map/pallas_call | solution.py:314
  58.1 1.9 %collective-permute-start.6 = (bf16[32,3584]{1,0:T(8,128)(2,1)S(1)}, bf16[32,3584]{1,0:T(8,128)(2,1)S(1)}, u32[]{:S(2)}, u32[]{:S(2)}) collective-permute-start(bf16[32,3584]{1,0:T(8,128)(2,1)S(1)} %get-tuple-element.64), channel_id=1, source_target_pairs={{0,8},{8,0},{16,24},{24,16},{32,40},{40,32},{48,56},{56,48},{64,72... | collective-permute-start | bytes 688136 | tf_op jit(solution)/shard_map/ppermute | solution.py:17
  60.1 2.1 %collective-permute-done.3.arrived = bf16[32,3584]{1,0:T(8,128)(2,1)S(1)} collective-permute-done((bf16[32,3584]{1,0:T(8,128)(2,1)S(1)}, bf16[32,3584]{1,0:T(8,128)(2,1)S(1)}, u32[]{:S(2)}, u32[]{:S(2)}) %collective-permute-start.3) | collective-permute-done | bytes 229408 | tf_op jit(solution)/shard_map/ppermute | solution.py:25
  62.2 3.1 %shard_map.129 = (bf16[32,3584]{1,0:T(8,128)(2,1)S(1)}, f32[32,256]{1,0:T(8,128)S(1)}) custom-call(s32[17]{0:T(128)S(1)} %get-tuple-element.42.scalars, bf16[32,3584]{1,0:T(8,128)(2,1)S(1)} %collective-permute-done.3.arrived, bf16[2,32,3584]{2,1,0:T(8,128)(2,1)S(1)} %bitcast.45, ...), custom_call_target="tpu_custom_call", output_to_operand_aliasing={{1}: (13, {})} | custom-call | flops 1000000 | bytes 1000 | tf_op jit(solution)/shard_map/pallas_call | solution.py:314
  65.3 1.9 %collective-permute-start.8 = (bf16[32,3584]{1,0:T(8,128)(2,1)S(1)}, bf16[32,3584]{1,0:T(8,128)(2,1)S(1)}, u32[]{:S(2)}, u32[]{:S(2)}) collective-permute-start(bf16[32,3584]{1,0:T(8,128)(2,1)S(1)} %get-tuple-element.71), channel_id=1, source_target_pairs={{0,8},{8,0},{16,24},{24,16},{32,40},{40,32},{48,56},{56,48},{64,72... | collective-permute-start | bytes 688136 | tf_op jit(solution)/shard_map/ppermute | solution.py:17
  67.2 0.0 collective-permute-done.6.arrived
  67.3 3.1 %shard_map.128 = (bf16[32,3584]{1,0:T(8,128)(2,1)S(1)}, f32[32,256]{1,0:T(8,128)S(1)}) custom-call(s32[17]{0:T(128)S(1)} %get-tuple-element.42.scalars, bf16[32,3584]{1,0:T(8,128)(2,1)S(1)} %collective-permute-done.6.arrived, bf16[2,32,3584]{2,1,0:T(8,128)(2,1)S(1)} %bitcast.46, ...), custom_call_target="tpu_custom_call", output_to_operand_aliasing={{1}: (13, {})} | custom-call | flops 1000000 | bytes 1000 | tf_op jit(solution)/shard_map/pallas_call | solution.py:314
  70.4 3.8 %collective-permute-start.9 = (bf16[32,3584]{1,0:T(8,128)(2,1)S(1)}, bf16[32,3584]{1,0:T(8,128)(2,1)S(1)}, u32[]{:S(2)}, u32[]{:S(2)}) collective-permute-start(bf16[32,3584]{1,0:T(8,128)(2,1)S(1)} %get-tuple-element.72), channel_id=1, source_target_pairs={{8,16},{16,8},{24,32},{32,24},{40,48},{48,40},{56,64},{64,56},{72,... | collective-permute-start | bytes 688136 | tf_op jit(solution)/shard_map/ppermute | solution.py:25
  74.1 5.4 %collective-permute-start.4 = (bf16[8,32,448]{2,1,0:T(8,128)(2,1)S(1)}, bf16[8,32,448]{2,1,0:T(8,128)(2,1)S(1)}, u32[]{:S(2)}, u32[]{:S(2)}) collective-permute-start(bf16[8,32,448]{2,1,0:T(8,128)(2,1)S(1)} %get-tuple-element.61), channel_id=1, source_target_pairs={{0,1016},{8,1008},{16,1000},{24,992},{32,984},{40,976},{48,968},{5... | collective-permute-start | bytes 688136 | tf_op jit(solution)/shard_map/ppermute | solution.py:30
  79.6 3.8 %collective-permute-start.7 = (bf16[32,256]{1,0:T(8,128)(2,1)S(1)}, bf16[32,256]{1,0:T(8,128)(2,1)S(1)}, u32[]{:S(2)}, u32[]{:S(2)}) collective-permute-start(bf16[32,256]{1,0:T(8,128)(2,1)S(1)} %get-tuple-element.70), channel_id=1, source_target_pairs={{0,1016},{8,1008},{16,1000},{24,992},{32,984},{40,976},{48,968},{5... | collective-permute-start | bytes 49160 | tf_op jit(solution)/shard_map/ppermute | solution.py:30
  83.4 42.1 %collective-permute-done.7.grads_upper = bf16[32,256]{1,0:T(8,128)(2,1)S(1)} collective-permute-done((bf16[32,256]{1,0:T(8,128)(2,1)S(1)}, bf16[32,256]{1,0:T(8,128)(2,1)S(1)}, u32[]{:S(2)}, u32[]{:S(2)}) %collective-permute-start.7) | collective-permute-done | bytes 16416 | tf_op jit(solution)/shard_map/ppermute | solution.py:30
  125.4 0.0 collective-permute-done.8.inner
  125.4 0.0 collective-permute-done.9.outer
  125.4 0.0 collective-permute-done.4.rows_upper
  125.4 1.0 shard_map.132
  126.5 5.8 %all-to-all-start = ((bf16[8,64,704]{2,1,0:T(8,128)(2,1)}), bf16[8,64,704]{2,1,0:T(8,128)(2,1)S(1)}, u32[]{:S(2)}, u32[]{:S(2)}) async-start(bf16[8,64,704]{2,1,0:T(8,128)(2,1)} %shard_map.132), calls=%async_computation | async-start | bytes 1572864 | tf_op jit(solution)/shard_map/all_to_all | solution.py:460
  132.2 0.8 shard_map.131
  133.0 9.0 %all-to-all-done.packed = bf16[8,64,704]{2,1,0:T(8,128)(2,1)S(1)} async-done(((bf16[8,64,704]{2,1,0:T(8,128)(2,1)}), bf16[8,64,704]{2,1,0:T(8,128)(2,1)S(1)}, u32[]{:S(2)}, u32[]{:S(2)}) %all-to-all-start) | async-done | bytes 720928 | tf_op jit(solution)/shard_map/all_to_all | solution.py:460
  142.0 1.2 shard_map.133
  (1 shorter events, 0.0 us)
Async XLA Ops:
  0.6 4.4 %copy-start.4 = (f32[1,2,2,256]{3,2,1,0:T(2,128)S(1)}, f32[1,2,2,256]{3,2,1,0:T(2,128)}, u32[]{:S(2)}) copy-start(f32[1,2,2,256]{3,2,1,0:T(2,128)} %param.16) | copy-start | bytes 12292
  0.6 4.4 %copy-start.3 = (f32[1,2,3584]{2,1,0:T(2,128)S(1)}, f32[1,2,3584]{2,1,0:T(2,128)}, u32[]{:S(2)}) copy-start(f32[1,2,3584]{2,1,0:T(2,128)} %param.15) | copy-start | bytes 86020
  0.7 4.4 %copy-start.2 = (bf16[2,1,2,16,3584]{4,3,2,1,0:T(8,128)(2,1)S(1)}, bf16[2,1,2,16,3584]{4,3,2,1,0:T(8,128)(2,1)}, u32[]{:S(2)}) copy-start(bf16[2,1,2,16,3584]{4,3,2,1,0:T(8,128)(2,1)} %param.12) | copy-start | bytes 1376260
  0.7 4.4 %copy-start = (bf16[1,2,3584,256]{3,2,1,0:T(8,128)(2,1)S(1)}, bf16[1,2,3584,256]{3,2,1,0:T(8,128)(2,1)}, u32[]{:S(2)}) copy-start(bf16[1,2,3584,256]{3,2,1,0:T(8,128)(2,1)} %param.13) | copy-start | bytes 11010052
  5.1 2.0 %copy-start.1 = (bf16[1,2,256,3584]{3,2,1,0:T(8,128)(2,1)S(1)}, bf16[1,2,256,3584]{3,2,1,0:T(8,128)(2,1)}, u32[]{:S(2)}) copy-start(bf16[1,2,256,3584]{3,2,1,0:T(8,128)(2,1)} %param.14) | copy-start | bytes 11010052
  10.2 23.8 %collective-permute-start = (bf16[32,3584]{1,0:T(8,128)(2,1)S(1)}, bf16[32,3584]{1,0:T(8,128)(2,1)S(1)}, u32[]{:S(2)}, u32[]{:S(2)}) collective-permute-start(bf16[32,3584]{1,0:T(8,128)(2,1)S(1)} %get-tuple-element.51), channel_id=1, source_target_pairs={{8,16},{16,8},{24,32},{32,24},{40,48},{48,40},{56,64},{64,56},{72,... | collective-permute-start | bytes 688136 | tf_op jit(solution)/shard_map/ppermute | solution.py:25
  32.1 7.5 %collective-permute-start.2 = (bf16[32,3584]{1,0:T(8,128)(2,1)S(1)}, bf16[32,3584]{1,0:T(8,128)(2,1)S(1)}, u32[]{:S(2)}, u32[]{:S(2)}) collective-permute-start(bf16[32,3584]{1,0:T(8,128)(2,1)S(1)} %get-tuple-element.56), channel_id=1, source_target_pairs={{0,8},{8,0},{16,24},{24,16},{32,40},{40,32},{48,56},{56,48},{64,72... | collective-permute-start | bytes 688136 | tf_op jit(solution)/shard_map/ppermute | solution.py:17
  37.2 11.0 %collective-permute-start.1 = (bf16[32,3584]{1,0:T(8,128)(2,1)S(1)}, bf16[32,3584]{1,0:T(8,128)(2,1)S(1)}, u32[]{:S(2)}, u32[]{:S(2)}) collective-permute-start(bf16[32,3584]{1,0:T(8,128)(2,1)S(1)} %get-tuple-element.55), channel_id=1, source_target_pairs={{0,8},{8,0},{16,24},{24,16},{32,40},{40,32},{48,56},{56,48},{64,72... | collective-permute-start | bytes 688136 | tf_op jit(solution)/shard_map/ppermute | solution.py:17
  42.7 12.3 %collective-permute-start.5 = (bf16[32,3584]{1,0:T(8,128)(2,1)S(1)}, bf16[32,3584]{1,0:T(8,128)(2,1)S(1)}, u32[]{:S(2)}, u32[]{:S(2)}) collective-permute-start(bf16[32,3584]{1,0:T(8,128)(2,1)S(1)} %get-tuple-element.62), channel_id=1, source_target_pairs={{8,16},{16,8},{24,32},{32,24},{40,48},{48,40},{56,64},{64,56},{72,... | collective-permute-start | bytes 688136 | tf_op jit(solution)/shard_map/ppermute | solution.py:25
  51.3 11.0 %collective-permute-start.3 = (bf16[32,3584]{1,0:T(8,128)(2,1)S(1)}, bf16[32,3584]{1,0:T(8,128)(2,1)S(1)}, u32[]{:S(2)}, u32[]{:S(2)}) collective-permute-start(bf16[32,3584]{1,0:T(8,128)(2,1)S(1)} %get-tuple-element.59), channel_id=1, source_target_pairs={{8,16},{16,8},{24,32},{32,24},{40,48},{48,40},{56,64},{64,56},{72,... | collective-permute-start | bytes 688136 | tf_op jit(solution)/shard_map/ppermute | solution.py:25
  58.1 9.1 %collective-permute-start.6 = (bf16[32,3584]{1,0:T(8,128)(2,1)S(1)}, bf16[32,3584]{1,0:T(8,128)(2,1)S(1)}, u32[]{:S(2)}, u32[]{:S(2)}) collective-permute-start(bf16[32,3584]{1,0:T(8,128)(2,1)S(1)} %get-tuple-element.64), channel_id=1, source_target_pairs={{0,8},{8,0},{16,24},{24,16},{32,40},{40,32},{48,56},{56,48},{64,72... | collective-permute-start | bytes 688136 | tf_op jit(solution)/shard_map/ppermute | solution.py:17
  65.3 60.1 %collective-permute-start.8 = (bf16[32,3584]{1,0:T(8,128)(2,1)S(1)}, bf16[32,3584]{1,0:T(8,128)(2,1)S(1)}, u32[]{:S(2)}, u32[]{:S(2)}) collective-permute-start(bf16[32,3584]{1,0:T(8,128)(2,1)S(1)} %get-tuple-element.71), channel_id=1, source_target_pairs={{0,8},{8,0},{16,24},{24,16},{32,40},{40,32},{48,56},{56,48},{64,72... | collective-permute-start | bytes 688136 | tf_op jit(solution)/shard_map/ppermute | solution.py:17
  70.4 55.1 %collective-permute-start.9 = (bf16[32,3584]{1,0:T(8,128)(2,1)S(1)}, bf16[32,3584]{1,0:T(8,128)(2,1)S(1)}, u32[]{:S(2)}, u32[]{:S(2)}) collective-permute-start(bf16[32,3584]{1,0:T(8,128)(2,1)S(1)} %get-tuple-element.72), channel_id=1, source_target_pairs={{8,16},{16,8},{24,32},{32,24},{40,48},{48,40},{56,64},{64,56},{72,... | collective-permute-start | bytes 688136 | tf_op jit(solution)/shard_map/ppermute | solution.py:25
  74.1 51.3 %collective-permute-start.4 = (bf16[8,32,448]{2,1,0:T(8,128)(2,1)S(1)}, bf16[8,32,448]{2,1,0:T(8,128)(2,1)S(1)}, u32[]{:S(2)}, u32[]{:S(2)}) collective-permute-start(bf16[8,32,448]{2,1,0:T(8,128)(2,1)S(1)} %get-tuple-element.61), channel_id=1, source_target_pairs={{0,1016},{8,1008},{16,1000},{24,992},{32,984},{40,976},{48,968},{5... | collective-permute-start | bytes 688136 | tf_op jit(solution)/shard_map/ppermute | solution.py:30
  79.6 45.9 %collective-permute-start.7 = (bf16[32,256]{1,0:T(8,128)(2,1)S(1)}, bf16[32,256]{1,0:T(8,128)(2,1)S(1)}, u32[]{:S(2)}, u32[]{:S(2)}) collective-permute-start(bf16[32,256]{1,0:T(8,128)(2,1)S(1)} %get-tuple-element.70), channel_id=1, source_target_pairs={{0,1016},{8,1008},{16,1000},{24,992},{32,984},{40,976},{48,968},{5... | collective-permute-start | bytes 49160 | tf_op jit(solution)/shard_map/ppermute | solution.py:30
  126.5 15.6 %all-to-all-start = ((bf16[8,64,704]{2,1,0:T(8,128)(2,1)}), bf16[8,64,704]{2,1,0:T(8,128)(2,1)S(1)}, u32[]{:S(2)}, u32[]{:S(2)}) async-start(bf16[8,64,704]{2,1,0:T(8,128)(2,1)} %shard_map.132), calls=%async_computation | async-start | bytes 1572864 | tf_op jit(solution)/shard_map/all_to_all | solution.py:460

commit v2 on v1

--- a/solution.py
+++ b/solution.py
@@ -137,9 +137,11 @@
         input_inverse_out[side] = jnp.broadcast_to(inverse, input_inverse_out.shape[1:])
         normed = (rows * inverse * gain_here[side : side + 1]).astype(jnp.bfloat16)
         all_normed.append(normed)
+        if side == 1:
+            to_mirror_out[...] = normed
+            continue
         for replica in range(replicas):
-            part = normed[:, replica * columns : (replica + 1) * columns]
-            (normed_out, to_mirror_out)[side][replica] = part
+            normed_out[replica] = normed[:, replica * columns : (replica + 1) * columns]
     for copy in others:
         copy.wait()
     scalars_out[0] = core
@@ -264,10 +266,12 @@
     )
 
 
-def own_grads_kernel(place, grads_zero, grads_one, lower, upper):
+def factors_kernel(place, grads_zero, grads_one, rows_upper, lower, upper):
     first = place[0] == 0
+    features = rows_upper.shape[1]
     lower[...] = jnp.where(first, grads_zero[...], grads_one[...]).astype(lower.dtype)
-    upper[...] = jnp.where(first, grads_one[...], grads_zero[...]).astype(upper.dtype)
+    upper[:, :features] = rows_upper[...]
+    upper[:, features:] = jnp.where(first, grads_one[...], grads_zero[...]).astype(upper.dtype)
 
 
 def own_states_kernel(place, inner, outer, forward_out, backward_out):
@@ -279,11 +283,14 @@
     backward_out[1 - core] = outer[row_count:]
 
 
-def pack_kernel(rows_lower, rows_upper, grads_lower, grads_upper, packed):
+def pack_kernel(rows_lower, grads_lower, upper, packed):
     replicas, block, columns = rows_lower.shape
+    grads_upper = upper[:, replicas * columns :]
     for replica in range(replicas):
         packed[replica, 0:block] = jnp.concatenate([rows_lower[replica], grads_lower[...]], axis=1)
-        packed[replica, block:] = jnp.concatenate([rows_upper[replica], grads_upper[...]], axis=1)
+        packed[replica, block:] = jnp.concatenate(
+            [upper[:, replica * columns : (replica + 1) * columns], grads_upper], axis=1
+        )
 
 
 def product_kernel(packed, result):
@@ -305,7 +312,9 @@
     return jax.ShapeDtypeStruct(shape, dtype)
 
 
-def call_kernel(kernel, outs, scalars, *operands, scalar_outs=0, in_hbm=(), scratch=(), aliases=()):
+def call_kernel(
+    kernel, outs, scalars, *operands, scalar_outs=0, in_hbm=(), scratch=(), aliases=(), moved=1000
+):
     specs = in_smem(len(scalars)) + in_vmem(len(operands))
     operands = list(operands)
     for at in in_hbm:
@@ -319,7 +328,7 @@
         scratch_shapes=scratch,
         input_output_aliases={len(scalars) + taken: given for taken, given in aliases},
         compiler_params=pltpu.CompilerParams(vmem_limit_bytes=vmem_limit),
-        cost_estimate=pl.CostEstimate(flops=1000000, bytes_accessed=1000, transcendentals=0),
+        cost_estimate=pl.CostEstimate(flops=1000000, bytes_accessed=moved, transcendentals=0),
     )(*scalars, *operands)
 
 
@@ -365,7 +374,7 @@
         [
             like(plan_at + sides * tick_count, dtype=jnp.int32),
             like(replicas, block, columns, dtype=narrow),
-            like(replicas, block, columns, dtype=narrow),
+            like(block, features, dtype=narrow),
             like(2 * row_count, features, dtype=narrow),
             like(2 * row_count, features, dtype=narrow),
             like(block, latent_width),
@@ -389,6 +398,7 @@
         gains_latent,
         scalar_outs=1,
         in_hbm=range(9),
+        moved=12000000,
         scratch=[
             pltpu.VMEM((sides, features, latent_width), narrow),
             pltpu.VMEM(stored.shape, stored.dtype),
@@ -429,34 +439,36 @@
 
     inner, outer, grads_zero, grads_one = carry
     for step in range(tick_count):
-        if step == tick_count - 1:
-            outer, to_mirror = lax.optimization_barrier((outer, to_mirror))
         to_outer, grads_zero = half_step(1, step, inner, grads_zero)
         to_inner, grads_one = half_step(0, step, outer, grads_one)
-        inner = with_chip_partner(to_inner)
-        outer = with_outer_partner(to_outer)
-
-    mirrored = from_mirror(to_mirror)
-    sums_lower, sums_upper = call_kernel(
-        own_grads_kernel,
-        [like(block, latent_width, dtype=narrow)] * 2,
+        if step < tick_count - 1:
+            inner = with_chip_partner(to_inner)
+            outer = with_outer_partner(to_outer)
+
+    sums_lower, upper = call_kernel(
+        factors_kernel,
+        [
+            like(block, latent_width, dtype=narrow),
+            like(block, features + latent_width, dtype=narrow),
+        ],
         [place],
         grads_zero,
         grads_one,
-    )
-    sums_mirrored = from_mirror(sums_upper)
-    mirrored, sums_mirrored, inner, outer = lax.optimization_barrier(
-        (mirrored, sums_mirrored, inner, outer)
-    )
+        to_mirror,
+    )
+    upper = from_mirror(upper)
+
     (packed,) = call_kernel(
         pack_kernel,
         [like(replicas, 2 * block, columns + latent_width, dtype=narrow)],
         [],
         normed,
-        mirrored,
         sums_lower,
-        sums_mirrored,
-    )
+        upper,
+    )
+    inner = with_chip_partner(to_inner)
+    outer = with_outer_partner(to_outer)
+    packed, inner, outer = lax.optimization_barrier((packed, inner, outer))
     packed = lax.all_to_all(packed, "dp", split_axis=0, concat_axis=0, tiled=True)
     (grad_down,) = call_kernel(product_kernel, [like(columns, latent_width)], [], packed)
     forward_out, backward_out = call_kernel(

time: 144 us -> 132 us (0.917)
  starting transfers between devices: 54.8 us -> 47.8 us
  waiting for transfers between devices: 53.3 us -> 48.7 us
    ppermute x2 -> x1, waiting for transfers between devices: 42.1 us -> 29.4 us  [from_mirror(): lax.ppermute(block, 'pipe', [(i, count - 1 - i) for i in range(count)])]
    ppermute x4, waiting for transfers between devices: 2.14 us -> 9.46 us  [with_outer_partner(): return lax.ppermute(block, 'pipe', pairs)]
    ppermute x2 -> x1, starting transfers between devices: 9.18 us -> 3.78 us  [from_mirror(): lax.ppermute(block, 'pipe', [(i, count - 1 - i) for i in range(count)])]
  transfers between devices with their start and end apart: 11 -> 10, of which waited for: 3 -> 5; matrix products, arithmetic and copies ran while one was open for 0% -> 0% of each run, Pallas kernels for 16% -> 16%
where the time goes in v2:
time: 132 us
  waiting for transfers between devices  48.7 us (37%)
  starting transfers between devices  47.8 us (36%)
  Pallas kernels  32.2 us (24%)
  local copies, waits for them, and re-layouts  2.05 us (2%)
    pallas_call x13, Pallas kernels, call_kernel(): pl.pallas_call(kernel, out_shape=outs, in_specs=specs, out_specs=in_smem(...  32.2 us
    ppermute x4, starting transfers between devices, with_outer_partner(): return lax.ppermute(block, 'pipe', pairs)  30.5 us
    ppermute x1, waiting for transfers between devices, from_mirror(): lax.ppermute(block, 'pipe', [(i, count - 1 - i) for i in range(count)])  29.4 us
    all_to_all x1, waiting for transfers between devices, shards(): lax.all_to_all(packed, 'dp', split_axis=0, concat_axis=0, tiled=True)  9.82 us
    ppermute x4, waiting for transfers between devices, with_outer_partner(): return lax.ppermute(block, 'pipe', pairs)  9.46 us
    ppermute x4, starting transfers between devices, with_chip_partner(): return lax.ppermute(block, 'pipe', [(i, i ^ 1) for i in range(count)])  7.68 us
    all_to_all x1, starting transfers between devices, shards(): lax.all_to_all(packed, 'dp', split_axis=0, concat_axis=0, tiled=True)  5.76 us
    ppermute x1, starting transfers between devices, from_mirror(): lax.ppermute(block, 'pipe', [(i, count - 1 - i) for i in range(count)])  3.78 us
  transfers between devices with their start and end apart: 10, of which 5 were waited for; matrix products, arithmetic and copies ran while one was open for 0% of the time, Pallas kernels for 16%

profile of v2, /device:TPU:24, one launch (start us, length us, event | category | flops | bytes accessed | tf_op | source)
XLA Modules:
  0.0 131.7 jit_solution(7888808584237999349)
XLA Ops:
  0.6 0.0 copy-start.4
  0.6 0.0 copy-start.3
  0.7 0.0 copy-start.2
  0.7 0.0 copy-start
  0.7 4.4 %shard_map.121 = (s32[17]{0:T(128)S(1)}, bf16[8,32,448]{2,1,0:T(8,128)(2,1)S(1)}, bf16[32,3584]{1,0:T(8,128)(2,1)S(1)}, bf16[32,3584]{1,0:T(8,128)(2,1)S(1)}, bf...) custom-call(s32[1]{0:T(128)} %bitcast.place, ...), custom_call_target="tpu_custom_call" | custom-call | flops 1000000 | bytes 12000000 | tf_op jit(solution)/shard_map/pallas_call | solution.py:323
  5.1 0.0 copy-done.4
  5.1 0.0 copy-done.3
  5.1 0.0 copy-done.2
  5.1 0.0 copy-done
  5.1 0.0 copy-start.1
  5.1 2.0 %copy-done.1 = bf16[1,2,256,3584]{3,2,1,0:T(8,128)(2,1)S(1)} copy-done((bf16[1,2,256,3584]{3,2,1,0:T(8,128)(2,1)S(1)}, bf16[1,2,256,3584]{3,2,1,0:T(8,128)(2,1)}, u32[]{:S(2)}) %copy-start.1) | copy-done | bytes 3670040
  7.1 3.1 %shard_map.122 = (bf16[32,3584]{1,0:T(8,128)(2,1)S(1)}, f32[32,256]{1,0:T(8,128)S(1)}) custom-call(s32[17]{0:T(128)S(1)} %get-tuple-element.40.scalars, bf16[32,3584]{1,0:T(8,128)(2,1)S(1)} %get-tuple-element.41.arrived, bf16[2,32,3584]{2,1,0:T(8,128)(2,1)S(1)} %bitcast.39, bf16[2,3584,256]{2,1,0:T(8,128)(2,1)S(1)} %bitcast.22, ...), custom_call_target="tpu_custom_call", output_to_operand_aliasing={{1}: (13, {})} | custom-call | flops 1000000 | bytes 1000 | tf_op jit(solution)/shard_map/pallas_call | solution.py:323
  10.2 1.9 %collective-permute-start = (bf16[32,3584]{1,0:T(8,128)(2,1)S(1)}, bf16[32,3584]{1,0:T(8,128)(2,1)S(1)}, u32[]{:S(2)}, u32[]{:S(2)}) collective-permute-start(bf16[32,3584]{1,0:T(8,128)(2,1)S(1)} %get-tuple-element.49), channel_id=1, source_target_pairs={{0,8},{8,0},{16,24},{24,16},{32,40},{40,32},{48,56},{56,48},{64,72... | collective-permute-start | bytes 688136 | tf_op jit(solution)/shard_map/ppermute | solution.py:17
  12.2 3.1 %shard_map.123 = (bf16[32,3584]{1,0:T(8,128)(2,1)S(1)}, f32[32,256]{1,0:T(8,128)S(1)}) custom-call(s32[17]{0:T(128)S(1)} %get-tuple-element.40.scalars, bf16[32,3584]{1,0:T(8,128)(2,1)S(1)} %get-tuple-element.50.arrived, bf16[2,32,3584]{2,1,0:T(8,128)(2,1)S(1)} %bitcast.40, bf16[2,3584,256]{2,1,0:T(8,128)(2,1)S(1)} %bitcast.23, ...), custom_call_target="tpu_custom_call", output_to_operand_aliasing={{1}: (13, {})} | custom-call | flops 1000000 | bytes 1000 | tf_op jit(solution)/shard_map/pallas_call | solution.py:323
  15.3 19.5 %collective-permute-start.2 = (bf16[32,3584]{1,0:T(8,128)(2,1)S(1)}, bf16[32,3584]{1,0:T(8,128)(2,1)S(1)}, u32[]{:S(2)}, u32[]{:S(2)}) collective-permute-start(bf16[32,3584]{1,0:T(8,128)(2,1)S(1)} %get-tuple-element.54), channel_id=1, source_target_pairs={{8,16},{16,8},{24,32},{32,24},{40,48},{48,40},{56,64},{64,56},{72,... | collective-permute-start | bytes 688136 | tf_op jit(solution)/shard_map/ppermute | solution.py:25
  34.7 0.0 collective-permute-done.arrived
  34.7 3.1 %shard_map.124 = (bf16[32,3584]{1,0:T(8,128)(2,1)S(1)}, f32[32,256]{1,0:T(8,128)S(1)}) custom-call(s32[17]{0:T(128)S(1)} %get-tuple-element.40.scalars, bf16[32,3584]{1,0:T(8,128)(2,1)S(1)} %collective-permute-done.arrived, bf16[2,32,3584]{2,1,0:T(8,128)(2,1)S(1)} %bitcast.41, bf16[2,3584,256]{2,1,0:T(8,128)(2,1)S(1)} %bitcast.24, ...), custom_call_target="tpu_custom_call", output_to_operand_aliasing={{1}: (13, {})} | custom-call | flops 1000000 | bytes 1000 | tf_op jit(solution)/shard_map/pallas_call | solution.py:323
  37.9 1.9 %collective-permute-start.1 = (bf16[32,3584]{1,0:T(8,128)(2,1)S(1)}, bf16[32,3584]{1,0:T(8,128)(2,1)S(1)}, u32[]{:S(2)}, u32[]{:S(2)}) collective-permute-start(bf16[32,3584]{1,0:T(8,128)(2,1)S(1)} %get-tuple-element.53), channel_id=1, source_target_pairs={{8,16},{16,8},{24,32},{32,24},{40,48},{48,40},{56,64},{64,56},{72,... | collective-permute-start | bytes 688136 | tf_op jit(solution)/shard_map/ppermute | solution.py:25
  39.8 0.0 collective-permute-done.2.arrived
  39.8 3.1 %shard_map.125 = (bf16[32,3584]{1,0:T(8,128)(2,1)S(1)}, f32[32,256]{1,0:T(8,128)S(1)}) custom-call(s32[17]{0:T(128)S(1)} %get-tuple-element.40.scalars, bf16[32,3584]{1,0:T(8,128)(2,1)S(1)} %collective-permute-done.2.arrived, bf16[2,32,3584]{2,1,0:T(8,128)(2,1)S(1)} %bitcast.42, ...), custom_call_target="tpu_custom_call", output_to_operand_aliasing={{1}: (13, {})} | custom-call | flops 1000000 | bytes 1000 | tf_op jit(solution)/shard_map/pallas_call | solution.py:323
  42.9 1.9 %collective-permute-start.4 = (bf16[32,3584]{1,0:T(8,128)(2,1)S(1)}, bf16[32,3584]{1,0:T(8,128)(2,1)S(1)}, u32[]{:S(2)}, u32[]{:S(2)}) collective-permute-start(bf16[32,3584]{1,0:T(8,128)(2,1)S(1)} %get-tuple-element.58), channel_id=1, source_target_pairs={{0,8},{8,0},{16,24},{24,16},{32,40},{40,32},{48,56},{56,48},{64,72... | collective-permute-start | bytes 688136 | tf_op jit(solution)/shard_map/ppermute | solution.py:17
  44.8 4.0 %collective-permute-done.1.arrived = bf16[32,3584]{1,0:T(8,128)(2,1)S(1)} collective-permute-done((bf16[32,3584]{1,0:T(8,128)(2,1)S(1)}, bf16[32,3584]{1,0:T(8,128)(2,1)S(1)}, u32[]{:S(2)}, u32[]{:S(2)}) %collective-permute-start.1) | collective-permute-done | bytes 229408 | tf_op jit(solution)/shard_map/ppermute | solution.py:25
  48.8 3.1 %shard_map.126 = (bf16[32,3584]{1,0:T(8,128)(2,1)S(1)}, f32[32,256]{1,0:T(8,128)S(1)}) custom-call(s32[17]{0:T(128)S(1)} %get-tuple-element.40.scalars, bf16[32,3584]{1,0:T(8,128)(2,1)S(1)} %collective-permute-done.1.arrived, bf16[2,32,3584]{2,1,0:T(8,128)(2,1)S(1)} %bitcast.43, ...), custom_call_target="tpu_custom_call", output_to_operand_aliasing={{1}: (13, {})} | custom-call | flops 1000000 | bytes 1000 | tf_op jit(solution)/shard_map/pallas_call | solution.py:323
  51.9 1.9 %collective-permute-start.3 = (bf16[32,3584]{1,0:T(8,128)(2,1)S(1)}, bf16[32,3584]{1,0:T(8,128)(2,1)S(1)}, u32[]{:S(2)}, u32[]{:S(2)}) collective-permute-start(bf16[32,3584]{1,0:T(8,128)(2,1)S(1)} %get-tuple-element.57), channel_id=1, source_target_pairs={{0,8},{8,0},{16,24},{24,16},{32,40},{40,32},{48,56},{56,48},{64,72... | collective-permute-start | bytes 688136 | tf_op jit(solution)/shard_map/ppermute | solution.py:17
  53.8 0.0 collective-permute-done.4.arrived
  53.8 3.1 %shard_map.127 = (bf16[32,3584]{1,0:T(8,128)(2,1)S(1)}, f32[32,256]{1,0:T(8,128)S(1)}) custom-call(s32[17]{0:T(128)S(1)} %get-tuple-element.40.scalars, bf16[32,3584]{1,0:T(8,128)(2,1)S(1)} %collective-permute-done.4.arrived, bf16[2,32,3584]{2,1,0:T(8,128)(2,1)S(1)} %bitcast.44, ...), custom_call_target="tpu_custom_call", output_to_operand_aliasing={{1}: (13, {})} | custom-call | flops 1000000 | bytes 1000 | tf_op jit(solution)/shard_map/pallas_call | solution.py:323
  57.0 3.8 %collective-permute-start.5 = (bf16[32,3584]{1,0:T(8,128)(2,1)S(1)}, bf16[32,3584]{1,0:T(8,128)(2,1)S(1)}, u32[]{:S(2)}, u32[]{:S(2)}) collective-permute-start(bf16[32,3584]{1,0:T(8,128)(2,1)S(1)} %get-tuple-element.62), channel_id=1, source_target_pairs={{8,16},{16,8},{24,32},{32,24},{40,48},{48,40},{56,64},{64,56},{72,... | collective-permute-start | bytes 688136 | tf_op jit(solution)/shard_map/ppermute | solution.py:25
  60.7 0.0 collective-permute-done.3.arrived
  60.7 3.1 %shard_map.128 = (bf16[32,3584]{1,0:T(8,128)(2,1)S(1)}, f32[32,256]{1,0:T(8,128)S(1)}) custom-call(s32[17]{0:T(128)S(1)} %get-tuple-element.40.scalars, bf16[32,3584]{1,0:T(8,128)(2,1)S(1)} %collective-permute-done.3.arrived, bf16[2,32,3584]{2,1,0:T(8,128)(2,1)S(1)} %bitcast.45, ...), custom_call_target="tpu_custom_call", output_to_operand_aliasing={{1}: (13, {})} | custom-call | flops 1000000 | bytes 1000 | tf_op jit(solution)/shard_map/pallas_call | solution.py:323
  63.9 4.1 %collective-permute-done.5.arrived = bf16[32,3584]{1,0:T(8,128)(2,1)S(1)} collective-permute-done((bf16[32,3584]{1,0:T(8,128)(2,1)S(1)}, bf16[32,3584]{1,0:T(8,128)(2,1)S(1)}, u32[]{:S(2)}, u32[]{:S(2)}) %collective-permute-start.5) | collective-permute-done | bytes 229408 | tf_op jit(solution)/shard_map/ppermute | solution.py:25
  67.9 3.1 %shard_map.129 = (bf16[32,3584]{1,0:T(8,128)(2,1)S(1)}, f32[32,256]{1,0:T(8,128)S(1)}) custom-call(s32[17]{0:T(128)S(1)} %get-tuple-element.40.scalars, bf16[32,3584]{1,0:T(8,128)(2,1)S(1)} %collective-permute-done.5.arrived, bf16[2,32,3584]{2,1,0:T(8,128)(2,1)S(1)} %bitcast.46, ...), custom_call_target="tpu_custom_call", output_to_operand_aliasing={{1}: (13, {})} | custom-call | flops 1000000 | bytes 1000 | tf_op jit(solution)/shard_map/pallas_call | solution.py:323
  71.0 3.8 %collective-permute-start.6 = (bf16[32,3840]{1,0:T(8,128)(2,1)S(1)}, bf16[32,3840]{1,0:T(8,128)(2,1)S(1)}, u32[]{:S(2)}, u32[]{:S(2)}) collective-permute-start(bf16[32,3840]{1,0:T(8,128)(2,1)S(1)} %get-tuple-element.67), channel_id=1, source_target_pairs={{0,1016},{8,1008},{16,1000},{24,992},{32,984},{40,976},{48,968},{5... | collective-permute-start | bytes 737288 | tf_op jit(solution)/shard_map/ppermute | solution.py:30
  74.8 5.4 %collective-permute-start.8 = (bf16[32,3584]{1,0:T(8,128)(2,1)S(1)}, bf16[32,3584]{1,0:T(8,128)(2,1)S(1)}, u32[]{:S(2)}, u32[]{:S(2)}) collective-permute-start(bf16[32,3584]{1,0:T(8,128)(2,1)S(1)} %get-tuple-element.69), channel_id=1, source_target_pairs={{8,16},{16,8},{24,32},{32,24},{40,48},{48,40},{56,64},{64,56},{72,... | collective-permute-start | bytes 688136 | tf_op jit(solution)/shard_map/ppermute | solution.py:25
  80.2 1.9 %collective-permute-start.7 = (bf16[32,3584]{1,0:T(8,128)(2,1)S(1)}, bf16[32,3584]{1,0:T(8,128)(2,1)S(1)}, u32[]{:S(2)}, u32[]{:S(2)}) collective-permute-start(bf16[32,3584]{1,0:T(8,128)(2,1)S(1)} %get-tuple-element.68), channel_id=1, source_target_pairs={{0,8},{8,0},{16,24},{24,16},{32,40},{40,32},{48,56},{56,48},{64,72... | collective-permute-start | bytes 688136 | tf_op jit(solution)/shard_map/ppermute | solution.py:17
  82.2 29.4 %collective-permute-done.6.upper = bf16[32,3840]{1,0:T(8,128)(2,1)S(1)} collective-permute-done((bf16[32,3840]{1,0:T(8,128)(2,1)S(1)}, bf16[32,3840]{1,0:T(8,128)(2,1)S(1)}, u32[]{:S(2)}, u32[]{:S(2)}) %collective-permute-start.6) | collective-permute-done | bytes 245792 | tf_op jit(solution)/shard_map/ppermute | solution.py:30
  111.6 1.0 shard_map.131
  112.6 1.4 %collective-permute-done.8.outer = bf16[32,3584]{1,0:T(8,128)(2,1)S(1)} collective-permute-done((bf16[32,3584]{1,0:T(8,128)(2,1)S(1)}, bf16[32,3584]{1,0:T(8,128)(2,1)S(1)}, u32[]{:S(2)}, u32[]{:S(2)}) %collective-permute-start.8) | collective-permute-done | bytes 229408 | tf_op jit(solution)/shard_map/ppermute | solution.py:25
  114.1 0.0 collective-permute-done.7.inner
  114.1 5.8 %all-to-all-start = ((bf16[8,64,704]{2,1,0:T(8,128)(2,1)}), bf16[8,64,704]{2,1,0:T(8,128)(2,1)S(1)}, u32[]{:S(2)}, u32[]{:S(2)}) async-start(bf16[8,64,704]{2,1,0:T(8,128)(2,1)} %shard_map.131), calls=%async_computation | async-start | bytes 1572864 | tf_op jit(solution)/shard_map/all_to_all | solution.py:472
  119.8 0.8 shard_map.132
  120.6 9.8 %all-to-all-done.packed = bf16[8,64,704]{2,1,0:T(8,128)(2,1)S(1)} async-done(((bf16[8,64,704]{2,1,0:T(8,128)(2,1)}), bf16[8,64,704]{2,1,0:T(8,128)(2,1)S(1)}, u32[]{:S(2)}, u32[]{:S(2)}) %all-to-all-start) | async-done | bytes 720928 | tf_op jit(solution)/shard_map/all_to_all | solution.py:472
  130.4 1.2 shard_map.133
  (1 shorter events, 0.0 us)
Async XLA Ops:
  0.6 4.4 %copy-start.4 = (f32[1,2,2,256]{3,2,1,0:T(2,128)S(1)}, f32[1,2,2,256]{3,2,1,0:T(2,128)}, u32[]{:S(2)}) copy-start(f32[1,2,2,256]{3,2,1,0:T(2,128)} %param.16) | copy-start | bytes 12292
  0.6 4.4 %copy-start.3 = (f32[1,2,3584]{2,1,0:T(2,128)S(1)}, f32[1,2,3584]{2,1,0:T(2,128)}, u32[]{:S(2)}) copy-start(f32[1,2,3584]{2,1,0:T(2,128)} %param.15) | copy-start | bytes 86020
  0.7 4.4 %copy-start.2 = (bf16[2,1,2,16,3584]{4,3,2,1,0:T(8,128)(2,1)S(1)}, bf16[2,1,2,16,3584]{4,3,2,1,0:T(8,128)(2,1)}, u32[]{:S(2)}) copy-start(bf16[2,1,2,16,3584]{4,3,2,1,0:T(8,128)(2,1)} %param.12) | copy-start | bytes 1376260
  0.7 4.4 %copy-start = (bf16[1,2,3584,256]{3,2,1,0:T(8,128)(2,1)S(1)}, bf16[1,2,3584,256]{3,2,1,0:T(8,128)(2,1)}, u32[]{:S(2)}) copy-start(bf16[1,2,3584,256]{3,2,1,0:T(8,128)(2,1)} %param.13) | copy-start | bytes 11010052
  5.1 2.0 %copy-start.1 = (bf16[1,2,256,3584]{3,2,1,0:T(8,128)(2,1)S(1)}, bf16[1,2,256,3584]{3,2,1,0:T(8,128)(2,1)}, u32[]{:S(2)}) copy-start(bf16[1,2,256,3584]{3,2,1,0:T(8,128)(2,1)} %param.14) | copy-start | bytes 11010052
  10.2 24.5 %collective-permute-start = (bf16[32,3584]{1,0:T(8,128)(2,1)S(1)}, bf16[32,3584]{1,0:T(8,128)(2,1)S(1)}, u32[]{:S(2)}, u32[]{:S(2)}) collective-permute-start(bf16[32,3584]{1,0:T(8,128)(2,1)S(1)} %get-tuple-element.49), channel_id=1, source_target_pairs={{0,8},{8,0},{16,24},{24,16},{32,40},{40,32},{48,56},{56,48},{64,72... | collective-permute-start | bytes 688136 | tf_op jit(solution)/shard_map/ppermute | solution.py:17
  15.3 24.5 %collective-permute-start.2 = (bf16[32,3584]{1,0:T(8,128)(2,1)S(1)}, bf16[32,3584]{1,0:T(8,128)(2,1)S(1)}, u32[]{:S(2)}, u32[]{:S(2)}) collective-permute-start(bf16[32,3584]{1,0:T(8,128)(2,1)S(1)} %get-tuple-element.54), channel_id=1, source_target_pairs={{8,16},{16,8},{24,32},{32,24},{40,48},{48,40},{56,64},{64,56},{72,... | collective-permute-start | bytes 688136 | tf_op jit(solution)/shard_map/ppermute | solution.py:25
  37.9 11.0 %collective-permute-start.1 = (bf16[32,3584]{1,0:T(8,128)(2,1)S(1)}, bf16[32,3584]{1,0:T(8,128)(2,1)S(1)}, u32[]{:S(2)}, u32[]{:S(2)}) collective-permute-start(bf16[32,3584]{1,0:T(8,128)(2,1)S(1)} %get-tuple-element.53), channel_id=1, source_target_pairs={{8,16},{16,8},{24,32},{32,24},{40,48},{48,40},{56,64},{64,56},{72,... | collective-permute-start | bytes 688136 | tf_op jit(solution)/shard_map/ppermute | solution.py:25
  42.9 10.9 %collective-permute-start.4 = (bf16[32,3584]{1,0:T(8,128)(2,1)S(1)}, bf16[32,3584]{1,0:T(8,128)(2,1)S(1)}, u32[]{:S(2)}, u32[]{:S(2)}) collective-permute-start(bf16[32,3584]{1,0:T(8,128)(2,1)S(1)} %get-tuple-element.58), channel_id=1, source_target_pairs={{0,8},{8,0},{16,24},{24,16},{32,40},{40,32},{48,56},{56,48},{64,72... | collective-permute-start | bytes 688136 | tf_op jit(solution)/shard_map/ppermute | solution.py:17
  51.9 8.8 %collective-permute-start.3 = (bf16[32,3584]{1,0:T(8,128)(2,1)S(1)}, bf16[32,3584]{1,0:T(8,128)(2,1)S(1)}, u32[]{:S(2)}, u32[]{:S(2)}) collective-permute-start(bf16[32,3584]{1,0:T(8,128)(2,1)S(1)} %get-tuple-element.57), channel_id=1, source_target_pairs={{0,8},{8,0},{16,24},{24,16},{32,40},{40,32},{48,56},{56,48},{64,72... | collective-permute-start | bytes 688136 | tf_op jit(solution)/shard_map/ppermute | solution.py:17
  57.0 11.0 %collective-permute-start.5 = (bf16[32,3584]{1,0:T(8,128)(2,1)S(1)}, bf16[32,3584]{1,0:T(8,128)(2,1)S(1)}, u32[]{:S(2)}, u32[]{:S(2)}) collective-permute-start(bf16[32,3584]{1,0:T(8,128)(2,1)S(1)} %get-tuple-element.62), channel_id=1, source_target_pairs={{8,16},{16,8},{24,32},{32,24},{40,48},{48,40},{56,64},{64,56},{72,... | collective-permute-start | bytes 688136 | tf_op jit(solution)/shard_map/ppermute | solution.py:25
  71.0 40.6 %collective-permute-start.6 = (bf16[32,3840]{1,0:T(8,128)(2,1)S(1)}, bf16[32,3840]{1,0:T(8,128)(2,1)S(1)}, u32[]{:S(2)}, u32[]{:S(2)}) collective-permute-start(bf16[32,3840]{1,0:T(8,128)(2,1)S(1)} %get-tuple-element.67), channel_id=1, source_target_pairs={{0,1016},{8,1008},{16,1000},{24,992},{32,984},{40,976},{48,968},{5... | collective-permute-start | bytes 737288 | tf_op jit(solution)/shard_map/ppermute | solution.py:30
  74.8 39.2 %collective-permute-start.8 = (bf16[32,3584]{1,0:T(8,128)(2,1)S(1)}, bf16[32,3584]{1,0:T(8,128)(2,1)S(1)}, u32[]{:S(2)}, u32[]{:S(2)}) collective-permute-start(bf16[32,3584]{1,0:T(8,128)(2,1)S(1)} %get-tuple-element.69), channel_id=1, source_target_pairs={{8,16},{16,8},{24,32},{32,24},{40,48},{48,40},{56,64},{64,56},{72,... | collective-permute-start | bytes 688136 | tf_op jit(solution)/shard_map/ppermute | solution.py:25
  80.2 33.8 %collective-permute-start.7 = (bf16[32,3584]{1,0:T(8,128)(2,1)S(1)}, bf16[32,3584]{1,0:T(8,128)(2,1)S(1)}, u32[]{:S(2)}, u32[]{:S(2)}) collective-permute-start(bf16[32,3584]{1,0:T(8,128)(2,1)S(1)} %get-tuple-element.68), channel_id=1, source_target_pairs={{0,8},{8,0},{16,24},{24,16},{32,40},{40,32},{48,56},{56,48},{64,72... | collective-permute-start | bytes 688136 | tf_op jit(solution)/shard_map/ppermute | solution.py:17
  114.1 16.4 %all-to-all-start = ((bf16[8,64,704]{2,1,0:T(8,128)(2,1)}), bf16[8,64,704]{2,1,0:T(8,128)(2,1)S(1)}, u32[]{:S(2)}, u32[]{:S(2)}) async-start(bf16[8,64,704]{2,1,0:T(8,128)(2,1)} %shard_map.131), calls=%async_computation | async-start | bytes 1572864 | tf_op jit(solution)/shard_map/all_to_all | solution.py:472

commit v3 on v2

--- a/solution.py
+++ b/solution.py
@@ -59,9 +59,12 @@
     forward_state,
     backward_state,
     w_down,
+    w_up,
     gain,
     latent_gain,
     scalars_out,
+    weights,
+    up_out,
     normed_out,
     to_mirror_out,
     inner_out,
@@ -74,7 +77,6 @@
     latent_inverse_out,
     input_inverse_out,
     probabilities_out,
-    weights,
     stored_here,
     gain_here,
     latent_gain_here,
@@ -85,6 +87,7 @@
     inputs_arrived,
     states_arrived,
     numbers_arrived,
+    up_arrived,
     *,
     forward_lengths_at,
     plan_at,
@@ -97,6 +100,7 @@
         pltpu.make_async_copy(w_down.at[side], weights.at[side], weights_arrived.at[side])
         for side in range(sides)
     ]
+    later = pltpu.make_async_copy(w_up, up_out, up_arrived)
     inputs = [
         pltpu.make_async_copy(source, target, inputs_arrived.at[at])
         for at, (source, target) in enumerate(
@@ -124,7 +128,7 @@
             )
         )
     ]
-    for copy in inputs + copies + others:
+    for copy in inputs + copies + others + [later]:
         copy.start()
     grads_zero_out[...] = jnp.zeros(grads_zero_out.shape, grads_zero_out.dtype)
     grads_one_out[...] = jnp.zeros(grads_one_out.shape, grads_one_out.dtype)
@@ -167,6 +171,7 @@
             probabilities_out[side, slot] = probabilities_of(
                 query_rows[part], key_rows[part], stored_lengths_here[side, 0, 0, slot]
             )
+    later.wait()
 
 
 def normed_rows(rows, gain_row):
@@ -369,10 +374,12 @@
         jnp.transpose(stored_lengths, (0, 1, 3, 2)),
     )
 
-    scalars, normed, to_mirror, *carry = call_kernel(
+    scalars, down_here, up_here, normed, to_mirror, *carry = call_kernel(
         functools.partial(prepare_kernel, forward_lengths_at=forward_lengths_at, plan_at=plan_at),
         [
             like(plan_at + sides * tick_count, dtype=jnp.int32),
+            like(*w_down.shape, dtype=narrow),
+            like(*w_up.shape, dtype=narrow),
             like(replicas, block, columns, dtype=narrow),
             like(block, features, dtype=narrow),
             like(2 * row_count, features, dtype=narrow),
@@ -394,13 +401,13 @@
         forward_state[:, 0],
         backward_state[:, 0],
         w_down,
+        w_up,
         gain,
         gains_latent,
         scalar_outs=1,
-        in_hbm=range(9),
+        in_hbm=range(10),
         moved=12000000,
         scratch=[
-            pltpu.VMEM((sides, features, latent_width), narrow),
             pltpu.VMEM(stored.shape, stored.dtype),
             pltpu.VMEM(gain.shape, gain.dtype),
             pltpu.VMEM(gains_latent.shape, gains_latent.dtype),
@@ -409,6 +416,7 @@
             pltpu.SemaphoreType.DMA((3,)),
             pltpu.SemaphoreType.DMA((4,)),
             pltpu.SemaphoreType.DMA((3,)),
+            pltpu.SemaphoreType.DMA,
         ],
     )
 
@@ -428,8 +436,8 @@
             [scalars],
             arrived,
             stored,
-            w_down,
-            w_up,
+            down_here,
+            up_here,
             gain,
             gains_latent,
             *kept,

time: 132 us -> 131 us (level)
  local copies, waits for them, and re-layouts: 2.05 us -> 0.01 us
    unnamed x10 -> x6, local copies, waits for them, and re-layouts: 2.05 us -> 0.01 us
where the time goes in v3:
time: 131 us; the launch traced here: 130 us
  waiting for transfers between devices  48.7 us (37%)
  starting transfers between devices  47.8 us (36%)
  Pallas kernels  32.7 us (25%)
    pallas_call x13, Pallas kernels, call_kernel(): pl.pallas_call(kernel, out_shape=outs, in_specs=specs, out_specs=in_smem(...  32.7 us
    ppermute x4, starting transfers between devices, with_outer_partner(): return lax.ppermute(block, 'pipe', pairs)  30.6 us
    ppermute x1, waiting for transfers between devices, from_mirror(): lax.ppermute(block, 'pipe', [(i, count - 1 - i) for i in range(count)])  29.4 us
    all_to_all x1, waiting for transfers between devices, shards(): lax.all_to_all(packed, 'dp', split_axis=0, concat_axis=0, tiled=True)  9.82 us
    ppermute x4, waiting for transfers between devices, with_outer_partner(): return lax.ppermute(block, 'pipe', pairs)  9.46 us
    ppermute x4, starting transfers between devices, with_chip_partner(): return lax.ppermute(block, 'pipe', [(i, i ^ 1) for i in range(count)])  7.68 us
    all_to_all x1, starting transfers between devices, shards(): lax.all_to_all(packed, 'dp', split_axis=0, concat_axis=0, tiled=True)  5.76 us
    ppermute x1, starting transfers between devices, from_mirror(): lax.ppermute(block, 'pipe', [(i, count - 1 - i) for i in range(count)])  3.78 us
  transfers between devices with their start and end apart: 10, of which 5 were waited for; matrix products, arithmetic and copies ran while one was open for 0% of the time, Pallas kernels for 16%

profile of v3, /device:TPU:24, one launch (start us, length us, event | category | flops | bytes accessed | tf_op | source)
XLA Modules:
  0.0 130.1 jit_solution(8132358922000546510)
XLA Ops:
  0.6 0.0 copy-start
  0.7 0.0 copy-start.1
  0.7 0.0 copy-start.2
  0.7 4.9 %shard_map.121 = (s32[17]{0:T(128)S(1)}, bf16[2,3584,256]{2,1,0:T(8,128)(2,1)S(1)}, bf16[2,256,3584]{2,1,0:T(8,128)(2,1)S(1)}, bf16[8,32,448]{2,1,0:T(8,128)(2,1...) custom-call(s32[1]{0:T(128)} %bitcast.place, ...), custom_call_target="tpu_custom_call" | custom-call | flops 1000000 | bytes 12000000 | tf_op jit(solution)/shard_map/pallas_call | solution.py:328
  5.6 0.0 copy-done
  5.6 0.0 copy-done.1
  5.6 0.0 copy-done.2
  5.6 3.1 %shard_map.122 = (bf16[32,3584]{1,0:T(8,128)(2,1)S(1)}, f32[32,256]{1,0:T(8,128)S(1)}) custom-call(s32[17]{0:T(128)S(1)} %get-tuple-element.42.scalars, bf16[32,3584]{1,0:T(8,128)(2,1)S(1)} %get-tuple-element.43.arrived, bf16[2,32,3584]{2,1,0:T(8,128)(2,1)S(1)} %bitcast.22, ...), custom_call_target="tpu_custom_call", output_to_operand_aliasing={{1}: (13, {})} | custom-call | flops 1000000 | bytes 1000 | tf_op jit(solution)/shard_map/pallas_call | solution.py:328
  8.7 1.9 %collective-permute-start = (bf16[32,3584]{1,0:T(8,128)(2,1)S(1)}, bf16[32,3584]{1,0:T(8,128)(2,1)S(1)}, u32[]{:S(2)}, u32[]{:S(2)}) collective-permute-start(bf16[32,3584]{1,0:T(8,128)(2,1)S(1)} %get-tuple-element.53), channel_id=1, source_target_pairs={{0,8},{8,0},{16,24},{24,16},{32,40},{40,32},{48,56},{56,48},{64,72... | collective-permute-start | bytes 688136 | tf_op jit(solution)/shard_map/ppermute | solution.py:17
  10.6 3.1 %shard_map.123 = (bf16[32,3584]{1,0:T(8,128)(2,1)S(1)}, f32[32,256]{1,0:T(8,128)S(1)}) custom-call(s32[17]{0:T(128)S(1)} %get-tuple-element.42.scalars, bf16[32,3584]{1,0:T(8,128)(2,1)S(1)} %get-tuple-element.54.arrived, bf16[2,32,3584]{2,1,0:T(8,128)(2,1)S(1)} %bitcast.23, ...), custom_call_target="tpu_custom_call", output_to_operand_aliasing={{1}: (13, {})} | custom-call | flops 1000000 | bytes 1000 | tf_op jit(solution)/shard_map/pallas_call | solution.py:328
  13.7 19.5 %collective-permute-start.2 = (bf16[32,3584]{1,0:T(8,128)(2,1)S(1)}, bf16[32,3584]{1,0:T(8,128)(2,1)S(1)}, u32[]{:S(2)}, u32[]{:S(2)}) collective-permute-start(bf16[32,3584]{1,0:T(8,128)(2,1)S(1)} %get-tuple-element.58), channel_id=1, source_target_pairs={{8,16},{16,8},{24,32},{32,24},{40,48},{48,40},{56,64},{64,56},{72,... | collective-permute-start | bytes 688136 | tf_op jit(solution)/shard_map/ppermute | solution.py:25
  33.2 0.0 collective-permute-done.arrived
  33.2 3.1 %shard_map.124 = (bf16[32,3584]{1,0:T(8,128)(2,1)S(1)}, f32[32,256]{1,0:T(8,128)S(1)}) custom-call(s32[17]{0:T(128)S(1)} %get-tuple-element.42.scalars, bf16[32,3584]{1,0:T(8,128)(2,1)S(1)} %collective-permute-done.arrived, bf16[2,32,3584]{2,1,0:T(8,128)(2,1)S(1)} %bitcast.24, ...), custom_call_target="tpu_custom_call", output_to_operand_aliasing={{1}: (13, {})} | custom-call | flops 1000000 | bytes 1000 | tf_op jit(solution)/shard_map/pallas_call | solution.py:328
  36.3 1.9 %collective-permute-start.1 = (bf16[32,3584]{1,0:T(8,128)(2,1)S(1)}, bf16[32,3584]{1,0:T(8,128)(2,1)S(1)}, u32[]{:S(2)}, u32[]{:S(2)}) collective-permute-start(bf16[32,3584]{1,0:T(8,128)(2,1)S(1)} %get-tuple-element.57), channel_id=1, source_target_pairs={{8,16},{16,8},{24,32},{32,24},{40,48},{48,40},{56,64},{64,56},{72,... | collective-permute-start | bytes 688136 | tf_op jit(solution)/shard_map/ppermute | solution.py:25
  38.2 0.0 collective-permute-done.2.arrived
  38.3 3.1 %shard_map.125 = (bf16[32,3584]{1,0:T(8,128)(2,1)S(1)}, f32[32,256]{1,0:T(8,128)S(1)}) custom-call(s32[17]{0:T(128)S(1)} %get-tuple-element.42.scalars, bf16[32,3584]{1,0:T(8,128)(2,1)S(1)} %collective-permute-done.2.arrived, bf16[2,32,3584]{2,1,0:T(8,128)(2,1)S(1)} %bitcast.25, ...), custom_call_target="tpu_custom_call", output_to_operand_aliasing={{1}: (13, {})} | custom-call | flops 1000000 | bytes 1000 | tf_op jit(solution)/shard_map/pallas_call | solution.py:328
  41.4 1.9 %collective-permute-start.4 = (bf16[32,3584]{1,0:T(8,128)(2,1)S(1)}, bf16[32,3584]{1,0:T(8,128)(2,1)S(1)}, u32[]{:S(2)}, u32[]{:S(2)}) collective-permute-start(bf16[32,3584]{1,0:T(8,128)(2,1)S(1)} %get-tuple-element.62), channel_id=1, source_target_pairs={{0,8},{8,0},{16,24},{24,16},{32,40},{40,32},{48,56},{56,48},{64,72... | collective-permute-start | bytes 688136 | tf_op jit(solution)/shard_map/ppermute | solution.py:17
  43.3 4.0 %collective-permute-done.1.arrived = bf16[32,3584]{1,0:T(8,128)(2,1)S(1)} collective-permute-done((bf16[32,3584]{1,0:T(8,128)(2,1)S(1)}, bf16[32,3584]{1,0:T(8,128)(2,1)S(1)}, u32[]{:S(2)}, u32[]{:S(2)}) %collective-permute-start.1) | collective-permute-done | bytes 229408 | tf_op jit(solution)/shard_map/ppermute | solution.py:25
  47.3 3.1 %shard_map.126 = (bf16[32,3584]{1,0:T(8,128)(2,1)S(1)}, f32[32,256]{1,0:T(8,128)S(1)}) custom-call(s32[17]{0:T(128)S(1)} %get-tuple-element.42.scalars, bf16[32,3584]{1,0:T(8,128)(2,1)S(1)} %collective-permute-done.1.arrived, bf16[2,32,3584]{2,1,0:T(8,128)(2,1)S(1)} %bitcast.26, ...), custom_call_target="tpu_custom_call", output_to_operand_aliasing={{1}: (13, {})} | custom-call | flops 1000000 | bytes 1000 | tf_op jit(solution)/shard_map/pallas_call | solution.py:328
  50.4 1.9 %collective-permute-start.3 = (bf16[32,3584]{1,0:T(8,128)(2,1)S(1)}, bf16[32,3584]{1,0:T(8,128)(2,1)S(1)}, u32[]{:S(2)}, u32[]{:S(2)}) collective-permute-start(bf16[32,3584]{1,0:T(8,128)(2,1)S(1)} %get-tuple-element.61), channel_id=1, source_target_pairs={{0,8},{8,0},{16,24},{24,16},{32,40},{40,32},{48,56},{56,48},{64,72... | collective-permute-start | bytes 688136 | tf_op jit(solution)/shard_map/ppermute | solution.py:17
  52.3 0.0 collective-permute-done.4.arrived
  52.3 3.1 %shard_map.127 = (bf16[32,3584]{1,0:T(8,128)(2,1)S(1)}, f32[32,256]{1,0:T(8,128)S(1)}) custom-call(s32[17]{0:T(128)S(1)} %get-tuple-element.42.scalars, bf16[32,3584]{1,0:T(8,128)(2,1)S(1)} %collective-permute-done.4.arrived, bf16[2,32,3584]{2,1,0:T(8,128)(2,1)S(1)} %bitcast.27, ...), custom_call_target="tpu_custom_call", output_to_operand_aliasing={{1}: (13, {})} | custom-call | flops 1000000 | bytes 1000 | tf_op jit(solution)/shard_map/pallas_call | solution.py:328
  55.4 3.8 %collective-permute-start.5 = (bf16[32,3584]{1,0:T(8,128)(2,1)S(1)}, bf16[32,3584]{1,0:T(8,128)(2,1)S(1)}, u32[]{:S(2)}, u32[]{:S(2)}) collective-permute-start(bf16[32,3584]{1,0:T(8,128)(2,1)S(1)} %get-tuple-element.66), channel_id=1, source_target_pairs={{8,16},{16,8},{24,32},{32,24},{40,48},{48,40},{56,64},{64,56},{72,... | collective-permute-start | bytes 688136 | tf_op jit(solution)/shard_map/ppermute | solution.py:25
  59.2 0.0 collective-permute-done.3.arrived
  59.2 3.1 %shard_map.128 = (bf16[32,3584]{1,0:T(8,128)(2,1)S(1)}, f32[32,256]{1,0:T(8,128)S(1)}) custom-call(s32[17]{0:T(128)S(1)} %get-tuple-element.42.scalars, bf16[32,3584]{1,0:T(8,128)(2,1)S(1)} %collective-permute-done.3.arrived, bf16[2,32,3584]{2,1,0:T(8,128)(2,1)S(1)} %bitcast.28, ...), custom_call_target="tpu_custom_call", output_to_operand_aliasing={{1}: (13, {})} | custom-call | flops 1000000 | bytes 1000 | tf_op jit(solution)/shard_map/pallas_call | solution.py:328
  62.3 4.1 %collective-permute-done.5.arrived = bf16[32,3584]{1,0:T(8,128)(2,1)S(1)} collective-permute-done((bf16[32,3584]{1,0:T(8,128)(2,1)S(1)}, bf16[32,3584]{1,0:T(8,128)(2,1)S(1)}, u32[]{:S(2)}, u32[]{:S(2)}) %collective-permute-start.5) | collective-permute-done | bytes 229408 | tf_op jit(solution)/shard_map/ppermute | solution.py:25
  66.4 3.1 %shard_map.129 = (bf16[32,3584]{1,0:T(8,128)(2,1)S(1)}, f32[32,256]{1,0:T(8,128)S(1)}) custom-call(s32[17]{0:T(128)S(1)} %get-tuple-element.42.scalars, bf16[32,3584]{1,0:T(8,128)(2,1)S(1)} %collective-permute-done.5.arrived, bf16[2,32,3584]{2,1,0:T(8,128)(2,1)S(1)} %bitcast.29, ...), custom_call_target="tpu_custom_call", output_to_operand_aliasing={{1}: (13, {})} | custom-call | flops 1000000 | bytes 1000 | tf_op jit(solution)/shard_map/pallas_call | solution.py:328
  69.5 3.8 %collective-permute-start.6 = (bf16[32,3840]{1,0:T(8,128)(2,1)S(1)}, bf16[32,3840]{1,0:T(8,128)(2,1)S(1)}, u32[]{:S(2)}, u32[]{:S(2)}) collective-permute-start(bf16[32,3840]{1,0:T(8,128)(2,1)S(1)} %get-tuple-element.71), channel_id=1, source_target_pairs={{0,1016},{8,1008},{16,1000},{24,992},{32,984},{40,976},{48,968},{5... | collective-permute-start | bytes 737288 | tf_op jit(solution)/shard_map/ppermute | solution.py:30
  73.3 5.4 %collective-permute-start.8 = (bf16[32,3584]{1,0:T(8,128)(2,1)S(1)}, bf16[32,3584]{1,0:T(8,128)(2,1)S(1)}, u32[]{:S(2)}, u32[]{:S(2)}) collective-permute-start(bf16[32,3584]{1,0:T(8,128)(2,1)S(1)} %get-tuple-element.73), channel_id=1, source_target_pairs={{8,16},{16,8},{24,32},{32,24},{40,48},{48,40},{56,64},{64,56},{72,... | collective-permute-start | bytes 688136 | tf_op jit(solution)/shard_map/ppermute | solution.py:25
  78.7 1.9 %collective-permute-start.7 = (bf16[32,3584]{1,0:T(8,128)(2,1)S(1)}, bf16[32,3584]{1,0:T(8,128)(2,1)S(1)}, u32[]{:S(2)}, u32[]{:S(2)}) collective-permute-start(bf16[32,3584]{1,0:T(8,128)(2,1)S(1)} %get-tuple-element.72), channel_id=1, source_target_pairs={{0,8},{8,0},{16,24},{24,16},{32,40},{40,32},{48,56},{56,48},{64,72... | collective-permute-start | bytes 688136 | tf_op jit(solution)/shard_map/ppermute | solution.py:17
  80.6 29.4 %collective-permute-done.6.upper = bf16[32,3840]{1,0:T(8,128)(2,1)S(1)} collective-permute-done((bf16[32,3840]{1,0:T(8,128)(2,1)S(1)}, bf16[32,3840]{1,0:T(8,128)(2,1)S(1)}, u32[]{:S(2)}, u32[]{:S(2)}) %collective-permute-start.6) | collective-permute-done | bytes 245792 | tf_op jit(solution)/shard_map/ppermute | solution.py:30
  110.1 1.0 shard_map.131
  111.1 1.4 %collective-permute-done.8.outer = bf16[32,3584]{1,0:T(8,128)(2,1)S(1)} collective-permute-done((bf16[32,3584]{1,0:T(8,128)(2,1)S(1)}, bf16[32,3584]{1,0:T(8,128)(2,1)S(1)}, u32[]{:S(2)}, u32[]{:S(2)}) %collective-permute-start.8) | collective-permute-done | bytes 229408 | tf_op jit(solution)/shard_map/ppermute | solution.py:25
  112.5 0.0 collective-permute-done.7.inner
  112.5 5.8 %all-to-all-start = ((bf16[8,64,704]{2,1,0:T(8,128)(2,1)}), bf16[8,64,704]{2,1,0:T(8,128)(2,1)S(1)}, u32[]{:S(2)}, u32[]{:S(2)}) async-start(bf16[8,64,704]{2,1,0:T(8,128)(2,1)} %shard_map.131), calls=%async_computation | async-start | bytes 1572864 | tf_op jit(solution)/shard_map/all_to_all | solution.py:480
  118.3 0.8 shard_map.132
  119.1 9.8 %all-to-all-done.packed = bf16[8,64,704]{2,1,0:T(8,128)(2,1)S(1)} async-done(((bf16[8,64,704]{2,1,0:T(8,128)(2,1)}), bf16[8,64,704]{2,1,0:T(8,128)(2,1)S(1)}, u32[]{:S(2)}, u32[]{:S(2)}) %all-to-all-start) | async-done | bytes 720928 | tf_op jit(solution)/shard_map/all_to_all | solution.py:480
  128.9 1.2 shard_map.133
  (1 shorter events, 0.0 us)
Async XLA Ops:
  0.6 4.9 %copy-start = (bf16[2,1,2,16,3584]{4,3,2,1,0:T(8,128)(2,1)S(1)}, bf16[2,1,2,16,3584]{4,3,2,1,0:T(8,128)(2,1)}, u32[]{:S(2)}) copy-start(bf16[2,1,2,16,3584]{4,3,2,1,0:T(8,128)(2,1)} %param.12) | copy-start | bytes 1376260
  0.7 4.9 %copy-start.1 = (f32[1,2,3584]{2,1,0:T(2,128)S(1)}, f32[1,2,3584]{2,1,0:T(2,128)}, u32[]{:S(2)}) copy-start(f32[1,2,3584]{2,1,0:T(2,128)} %param.15) | copy-start | bytes 86020
  0.7 4.9 %copy-start.2 = (f32[1,2,2,256]{3,2,1,0:T(2,128)S(1)}, f32[1,2,2,256]{3,2,1,0:T(2,128)}, u32[]{:S(2)}) copy-start(f32[1,2,2,256]{3,2,1,0:T(2,128)} %param.16) | copy-start | bytes 12292
  8.7 24.5 %collective-permute-start = (bf16[32,3584]{1,0:T(8,128)(2,1)S(1)}, bf16[32,3584]{1,0:T(8,128)(2,1)S(1)}, u32[]{:S(2)}, u32[]{:S(2)}) collective-permute-start(bf16[32,3584]{1,0:T(8,128)(2,1)S(1)} %get-tuple-element.53), channel_id=1, source_target_pairs={{0,8},{8,0},{16,24},{24,16},{32,40},{40,32},{48,56},{56,48},{64,72... | collective-permute-start | bytes 688136 | tf_op jit(solution)/shard_map/ppermute | solution.py:17
  13.7 24.5 %collective-permute-start.2 = (bf16[32,3584]{1,0:T(8,128)(2,1)S(1)}, bf16[32,3584]{1,0:T(8,128)(2,1)S(1)}, u32[]{:S(2)}, u32[]{:S(2)}) collective-permute-start(bf16[32,3584]{1,0:T(8,128)(2,1)S(1)} %get-tuple-element.58), channel_id=1, source_target_pairs={{8,16},{16,8},{24,32},{32,24},{40,48},{48,40},{56,64},{64,56},{72,... | collective-permute-start | bytes 688136 | tf_op jit(solution)/shard_map/ppermute | solution.py:25
  36.3 11.0 %collective-permute-start.1 = (bf16[32,3584]{1,0:T(8,128)(2,1)S(1)}, bf16[32,3584]{1,0:T(8,128)(2,1)S(1)}, u32[]{:S(2)}, u32[]{:S(2)}) collective-permute-start(bf16[32,3584]{1,0:T(8,128)(2,1)S(1)} %get-tuple-element.57), channel_id=1, source_target_pairs={{8,16},{16,8},{24,32},{32,24},{40,48},{48,40},{56,64},{64,56},{72,... | collective-permute-start | bytes 688136 | tf_op jit(solution)/shard_map/ppermute | solution.py:25
  41.4 10.9 %collective-permute-start.4 = (bf16[32,3584]{1,0:T(8,128)(2,1)S(1)}, bf16[32,3584]{1,0:T(8,128)(2,1)S(1)}, u32[]{:S(2)}, u32[]{:S(2)}) collective-permute-start(bf16[32,3584]{1,0:T(8,128)(2,1)S(1)} %get-tuple-element.62), channel_id=1, source_target_pairs={{0,8},{8,0},{16,24},{24,16},{32,40},{40,32},{48,56},{56,48},{64,72... | collective-permute-start | bytes 688136 | tf_op jit(solution)/shard_map/ppermute | solution.py:17
  50.4 8.8 %collective-permute-start.3 = (bf16[32,3584]{1,0:T(8,128)(2,1)S(1)}, bf16[32,3584]{1,0:T(8,128)(2,1)S(1)}, u32[]{:S(2)}, u32[]{:S(2)}) collective-permute-start(bf16[32,3584]{1,0:T(8,128)(2,1)S(1)} %get-tuple-element.61), channel_id=1, source_target_pairs={{0,8},{8,0},{16,24},{24,16},{32,40},{40,32},{48,56},{56,48},{64,72... | collective-permute-start | bytes 688136 | tf_op jit(solution)/shard_map/ppermute | solution.py:17
  55.4 11.0 %collective-permute-start.5 = (bf16[32,3584]{1,0:T(8,128)(2,1)S(1)}, bf16[32,3584]{1,0:T(8,128)(2,1)S(1)}, u32[]{:S(2)}, u32[]{:S(2)}) collective-permute-start(bf16[32,3584]{1,0:T(8,128)(2,1)S(1)} %get-tuple-element.66), channel_id=1, source_target_pairs={{8,16},{16,8},{24,32},{32,24},{40,48},{48,40},{56,64},{64,56},{72,... | collective-permute-start | bytes 688136 | tf_op jit(solution)/shard_map/ppermute | solution.py:25
  69.5 40.6 %collective-permute-start.6 = (bf16[32,3840]{1,0:T(8,128)(2,1)S(1)}, bf16[32,3840]{1,0:T(8,128)(2,1)S(1)}, u32[]{:S(2)}, u32[]{:S(2)}) collective-permute-start(bf16[32,3840]{1,0:T(8,128)(2,1)S(1)} %get-tuple-element.71), channel_id=1, source_target_pairs={{0,1016},{8,1008},{16,1000},{24,992},{32,984},{40,976},{48,968},{5... | collective-permute-start | bytes 737288 | tf_op jit(solution)/shard_map/ppermute | solution.py:30
  73.3 39.2 %collective-permute-start.8 = (bf16[32,3584]{1,0:T(8,128)(2,1)S(1)}, bf16[32,3584]{1,0:T(8,128)(2,1)S(1)}, u32[]{:S(2)}, u32[]{:S(2)}) collective-permute-start(bf16[32,3584]{1,0:T(8,128)(2,1)S(1)} %get-tuple-element.73), channel_id=1, source_target_pairs={{8,16},{16,8},{24,32},{32,24},{40,48},{48,40},{56,64},{64,56},{72,... | collective-permute-start | bytes 688136 | tf_op jit(solution)/shard_map/ppermute | solution.py:25
  78.7 33.8 %collective-permute-start.7 = (bf16[32,3584]{1,0:T(8,128)(2,1)S(1)}, bf16[32,3584]{1,0:T(8,128)(2,1)S(1)}, u32[]{:S(2)}, u32[]{:S(2)}) collective-permute-start(bf16[32,3584]{1,0:T(8,128)(2,1)S(1)} %get-tuple-element.72), channel_id=1, source_target_pairs={{0,8},{8,0},{16,24},{24,16},{32,40},{40,32},{48,56},{56,48},{64,72... | collective-permute-start | bytes 688136 | tf_op jit(solution)/shard_map/ppermute | solution.py:17
  112.5 16.4 %all-to-all-start = ((bf16[8,64,704]{2,1,0:T(8,128)(2,1)}), bf16[8,64,704]{2,1,0:T(8,128)(2,1)S(1)}, u32[]{:S(2)}, u32[]{:S(2)}) async-start(bf16[8,64,704]{2,1,0:T(8,128)(2,1)} %shard_map.131), calls=%async_computation | async-start | bytes 1572864 | tf_op jit(solution)/shard_map/all_to_all | solution.py:480
